TPU v7x, 256 devices: a whole 4x4x8 slice. The times are simulated.
256 devices in a mesh: dp: 2 (over x_lo), tile: 128 (over z, y, x_hi, core).
Axes of the slice: x: 4 (x_hi: 2, x_lo: 2; x = x_hi * 2 + x_lo), y: 4, z: 8, core: 2. Of those that a mesh axis runs over, the one named last changes fastest.
Arguments:
- features: bfloat16 [8, 2, 16384, 1024], P('dp', None, 'tile'), may hold values from -6 to 6
- proj_weight: bfloat16 [2, 1024, 256], replicated, may hold values from -0.1875 to 0.1875
- conv_weight: bfloat16 [2, 3, 3, 256, 256], replicated, may hold values from -0.125 to 0.125
- saved: bfloat16 [8, 2, 1024, 16, 256], P('dp', None, 'tile'), may hold values from -6 to 6
- cotangent: bfloat16 [8, 2048, 32, 256], P('dp', 'tile'), may hold values from -6 to 6
Outputs:
- feature_grad: bfloat16 [8, 2, 16384, 1024], P('dp', None, 'tile')
- head_grad: float32 [6656, 256], P(('dp', 'tile'))
All inputs are finite; a program needn't handle non-finite values.
Results may differ from a plain program's by a relative error of at most 0.0057.
Values may be sent and summed in bfloat16 or wider, within the bound.
A program may use at most 128 MiB of HBM per device.

v0:
```python
import math

import jax
import jax.numpy as jnp
from jax import lax
from jax.sharding import PartitionSpec as P

COL_BITS = 3
TILE_COLS = 8


def from_partner(block, axis, apart):
    count = lax.axis_size(axis)
    route = []
    for low in range(count):
        high = low | 1 << apart
        if high != low and high < count:
            route += [(low, high), (high, low)]
    return lax.ppermute(block, axis, route)


def from_behind(block, axis, distance):
    devices = range(lax.axis_size(axis))
    route = [(i - distance, i) for i in devices if i - distance in devices]
    return lax.ppermute(block, axis, route)


def pool(values_in, along_dim, lo_edge, hi_edge):
    cell_count = (values_in.shape[along_dim] - 2) // 2
    even_part = lax.slice_in_dim(values_in, 1, 2 * cell_count + 1, 2, along_dim)
    odd_part = lax.slice_in_dim(values_in, 2, 2 * cell_count + 2, 2, along_dim)
    before = lax.slice_in_dim(values_in, 0, 2 * cell_count, 2, along_dim)
    after = lax.slice_in_dim(values_in, 3, 2 * cell_count + 2, 2, along_dim)
    target_shape = [1] * values_in.ndim
    target_shape[along_dim] = cell_count
    iota_pos = lax.broadcasted_iota(jnp.int32, tuple(target_shape), along_dim)
    at_first = jnp.logical_and(iota_pos == 0, lo_edge)
    at_last = jnp.logical_and(iota_pos == cell_count - 1, hi_edge)
    result = 0.75 * (even_part + odd_part) + 0.25 * (before + after)
    result = result + 0.25 * jnp.where(at_first, even_part, jnp.zeros_like(even_part))
    result = result + 0.25 * jnp.where(at_last, odd_part, jnp.zeros_like(odd_part))
    return result


def column_of(code):
    column = code
    for step_bit in range(1, COL_BITS):
        column = jnp.bitwise_xor(column, jnp.right_shift(code, step_bit))
    return column


def trade(outgoing, bit_index):
    return from_partner(outgoing, "tile", bit_index)


def widen(field_in, col_pos, gray_pos):
    width = field_in.shape[2]
    left_edge = field_in[:, :, :1]
    right_edge = field_in[:, :, width - 1 :]
    left_rim = jnp.zeros_like(left_edge)
    right_rim = jnp.zeros_like(right_edge)
    for bit_index in range(COL_BITS):
        partner_col = column_of(jnp.bitwise_xor(gray_pos, 1 << bit_index))
        to_left = partner_col == col_pos - 1
        to_right = partner_col == col_pos + 1
        outgoing = jnp.where(
            to_left, left_edge, jnp.where(to_right, right_edge, jnp.zeros_like(left_edge))
        )
        incoming = trade(outgoing, bit_index)
        left_rim = jnp.where(to_left, incoming, left_rim)
        right_rim = jnp.where(to_right, incoming, right_rim)
    side = jnp.concatenate([left_rim, field_in, right_rim], axis=2)
    upper = from_behind(side[:, side.shape[1] - 1 :], "tile", TILE_COLS)
    lower = from_behind(side[:, :1], "tile", -TILE_COLS)
    return jnp.concatenate([upper, side, lower], axis=1)


def regroup(grouped, gray_pos, sender):
    full_shape = grouped.shape
    for bit_index in range(COL_BITS):
        half_size = 1 << bit_index
        split_view = grouped.reshape(
            full_shape[0],
            full_shape[1],
            TILE_COLS // (2 * half_size),
            2,
            half_size,
            full_shape[3],
            full_shape[4],
            full_shape[5],
        )
        lower_half = split_view[:, :, :, 0]
        upper_half = split_view[:, :, :, 1]
        mine_low = gray_pos // half_size % 2 == 0
        outgoing = jnp.where(mine_low, upper_half, lower_half)
        kept_half = jnp.where(mine_low, lower_half, upper_half)
        incoming = sender(outgoing, bit_index)
        new_lower = jnp.where(mine_low, kept_half, incoming)
        new_upper = jnp.where(mine_low, incoming, kept_half)
        grouped = jnp.stack([new_lower, new_upper], axis=3).reshape(full_shape)
    order = [column ^ column >> 1 for column in range(TILE_COLS)]
    grouped = jnp.take(grouped, jnp.array(order, jnp.int32), axis=2)
    ordered = grouped.transpose(0, 1, 3, 2, 4, 5)
    return ordered.reshape(
        full_shape[0], full_shape[1], full_shape[3] * full_shape[2] * full_shape[4], full_shape[5]
    )


def send_each(outgoing, bit_index):
    return from_partner(outgoing, "tile", bit_index)


def project(token_grad, weights, feats):
    feat_grad = jnp.einsum(
        "iknc,kdc->iknd", token_grad, weights, preferred_element_type=jnp.float32
    )
    proj_term = jnp.einsum("iknd,iknc->kdc", feats, token_grad, preferred_element_type=jnp.float32)
    return (feat_grad.astype(jnp.bfloat16), proj_term.reshape(-1, token_grad.shape[3]))


def per_device(features, proj_weight, conv_weight, saved, cotangent):
    position = lax.axis_index("tile")
    gray_pos = position % TILE_COLS
    col_pos = column_of(gray_pos)
    row_pos = position // TILE_COLS
    row_count = lax.axis_size("tile") // TILE_COLS
    image_count = features.shape[0]
    depth_count = features.shape[1]
    tok_dev = features.shape[2]
    tile_height = saved.shape[2]
    tile_width = saved.shape[3]
    channels = saved.shape[4]
    padded_grad = widen(cotangent, col_pos, gray_pos).astype(jnp.float32)
    row_pooled = pool(padded_grad, 1, row_pos == 0, row_pos == row_count - 1)
    pooled = pool(row_pooled, 2, col_pos == 0, col_pos == TILE_COLS - 1).astype(jnp.bfloat16)
    dpad = widen(pooled, col_pos, gray_pos)
    shifted = [
        dpad[
            :,
            2 - kernel_row : 2 - kernel_row + tile_height,
            2 - kernel_col : 2 - kernel_col + tile_width,
        ]
        for kernel_row in range(3)
        for kernel_col in range(3)
    ]
    patches = jnp.stack(shifted, axis=3).reshape(
        image_count, tile_height, tile_width, 3, 3, channels
    )
    input_grad = jnp.einsum(
        "ihwuvo,kuvco->ikhwc", patches, conv_weight, preferred_element_type=jnp.float32
    ).astype(jnp.bfloat16)
    conv_term = jnp.einsum(
        "ikhwc,ihwuvo->kuvco", saved, patches, preferred_element_type=jnp.float32
    ).reshape(-1, channels)
    grouped = input_grad.reshape(
        image_count, depth_count, TILE_COLS, tile_height // TILE_COLS, tile_width, channels
    )
    grad_parts = []
    term_parts = []
    for depth_index in range(depth_count):
        token_grad = regroup(grouped[:, depth_index : depth_index + 1], gray_pos, send_each)
        feat_part, term_part = project(
            token_grad,
            proj_weight[depth_index : depth_index + 1],
            features[:, depth_index : depth_index + 1],
        )
        grad_parts.append(feat_part)
        term_parts.append(term_part)
    feature_grad = jnp.concatenate(grad_parts, axis=1)
    proj_term = jnp.concatenate(term_parts, axis=0)
    scale = 1.0 / math.sqrt(image_count * lax.axis_size("dp") * tok_dev * lax.axis_size("tile"))
    head_terms = jnp.concatenate([proj_term, conv_term], axis=0) * scale
    head_grad = lax.psum_scatter(head_terms, ("dp", "tile"), scatter_dimension=0, tiled=True)
    return (feature_grad, head_grad)


def solution(mesh):
    in_specs = (
        P("dp", None, "tile", None),
        P(),
        P(),
        P("dp", None, "tile", None, None),
        P("dp", "tile", None, None),
    )
    out_specs = (P("dp", None, "tile", None), P(("dp", "tile"), None))
    return jax.shard_map(
        per_device, mesh=mesh, in_specs=in_specs, out_specs=out_specs, check_vma=False
    )
```

profile of v0, /device:TPU:1, one launch (start us, length us, event | category | flops | bytes accessed | tf_op | source)
XLA Modules:
  0.0 1242.7 jit_solution(14490348301278364724)
XLA Ops:
  11.9 4.5 collective-permute-start.3
  17.9 5.2 collective-permute-done.4
  25.3 3.8 slice.142
  29.1 5.1 slice.143
  34.3 5.0 slice.144
  39.3 5.1 slice.145
  49.1 3.9 collective-permute-start.7
  55.3 6.1 collective-permute-start.9
  67.7 17.8 %collective-permute-start.13 = (bf16[4,1,4,1,1,16,256]{6,5,2,0,4,3,1:T(8,128)(2,1)S(1)}, bf16[4,1,4,1,1,16,256]{6,5,2,0,4,3,1:T(8,128)(2,1)S(1)}, u32[]{:S(2)}, u32[]{:S(2)}) collective-permute-start(bf16[4,1,4,1,1,16,256]{6,5,2,0,4,3,1:T(8,128)(2,1)S(1)} %fusion.35), channel_id=1, source_target_pairs={{0,1},{1,0},{2,3},{3,2},{4,5},{5,4},{6,7},{7,6},{8,9},{9,8},{10,11... | collective-permute-start | bytes 393224 | tf_op jit(solution)/shard_map/ppermute | solution.py:19
  85.5 3.7 fusion.3
  89.3 3.0 collective-permute-start.11
  92.3 10.4 collective-permute-start.14
  104.3 4.9 collective-permute-done.14
  110.0 10.3 collective-permute-start.15
  130.8 5.0 maximum_multiply_fusion
  135.9 694.7 %fusion = f32[32,256]{1,0:T(8,128)S(1)} fusion(f32[6656,256]{1,0:T(8,128)} %maximum_multiply_fusion), kind=kCustom, calls=%all-reduce-scatter | all-reduce-scatter fusion | flops 2097153 | bytes 6848512
  830.6 25.4 %collective-permute-start.16 = (f32[32,256]{1,0:T(8,128)S(1)}, f32[32,256]{1,0:T(8,128)S(1)}, u32[]{:S(2)}, u32[]{:S(2)}) collective-permute-start(f32[32,256]{1,0:T(8,128)S(1)} %fusion), channel_id=1, source_target_pairs={{0,1},{1,2},{2,3},{3,4},{4,5},{5,6},{6,7},{7,8},{8,9},{9,10},{10,1... | collective-permute-start | bytes 98312
  856.0 13.1 %collective-permute-start.17 = (f32[32,256]{1,0:T(8,128)S(1)}, f32[32,256]{1,0:T(8,128)S(1)}, u32[]{:S(2)}, u32[]{:S(2)}) collective-permute-start(f32[32,256]{1,0:T(8,128)S(1)} %fusion), channel_id=1, source_target_pairs={{0,2},{1,3},{2,4},{3,5},{4,6},{5,7},{6,8},{7,9},{8,10},{9,11},{10,... | collective-permute-start | bytes 98312
  869.2 5.8 collective-permute-start.63
  874.9 10.7 collective-permute-start.18
  885.6 13.1 %collective-permute-start.19 = (f32[32,256]{1,0:T(8,128)S(1)}, f32[32,256]{1,0:T(8,128)S(1)}, u32[]{:S(2)}, u32[]{:S(2)}) collective-permute-start(f32[32,256]{1,0:T(8,128)S(1)} %fusion), channel_id=1, source_target_pairs={{0,4},{1,5},{2,6},{3,7},{4,8},{5,9},{6,10},{7,11},{8,12},{9,13},{1... | collective-permute-start | bytes 98312
  898.7 13.1 %collective-permute-start.20 = (f32[32,256]{1,0:T(8,128)S(1)}, f32[32,256]{1,0:T(8,128)S(1)}, u32[]{:S(2)}, u32[]{:S(2)}) collective-permute-start(f32[32,256]{1,0:T(8,128)S(1)} %fusion), channel_id=1, source_target_pairs={{0,5},{1,6},{2,7},{3,8},{4,9},{5,10},{6,11},{7,12},{8,13},{9,14},{... | collective-permute-start | bytes 98312
  911.8 13.1 %collective-permute-start.21 = (f32[32,256]{1,0:T(8,128)S(1)}, f32[32,256]{1,0:T(8,128)S(1)}, u32[]{:S(2)}, u32[]{:S(2)}) collective-permute-start(f32[32,256]{1,0:T(8,128)S(1)} %fusion), channel_id=1, source_target_pairs={{0,6},{1,7},{2,8},{3,9},{4,10},{5,11},{6,12},{7,13},{8,14},{9,15},... | collective-permute-start | bytes 98312
  925.0 13.1 %collective-permute-start.22 = (f32[32,256]{1,0:T(8,128)S(1)}, f32[32,256]{1,0:T(8,128)S(1)}, u32[]{:S(2)}, u32[]{:S(2)}) collective-permute-start(f32[32,256]{1,0:T(8,128)S(1)} %fusion), channel_id=1, source_target_pairs={{0,7},{1,8},{2,9},{3,10},{4,11},{5,12},{6,13},{7,14},{8,15},{9,16}... | collective-permute-start | bytes 98312
  938.1 13.1 %collective-permute-start.23 = (f32[32,256]{1,0:T(8,128)S(1)}, f32[32,256]{1,0:T(8,128)S(1)}, u32[]{:S(2)}, u32[]{:S(2)}) collective-permute-start(f32[32,256]{1,0:T(8,128)S(1)} %fusion), channel_id=1, source_target_pairs={{0,8},{1,9},{2,10},{3,11},{4,12},{5,13},{6,14},{7,15},{8,16},{9,17... | collective-permute-start | bytes 98312
  951.3 13.1 %collective-permute-start.24 = (f32[32,256]{1,0:T(8,128)S(1)}, f32[32,256]{1,0:T(8,128)S(1)}, u32[]{:S(2)}, u32[]{:S(2)}) collective-permute-start(f32[32,256]{1,0:T(8,128)S(1)} %fusion), channel_id=1, source_target_pairs={{0,9},{1,10},{2,11},{3,12},{4,13},{5,14},{6,15},{7,16},{8,17},{9,1... | collective-permute-start | bytes 98312
  964.4 13.1 %collective-permute-start.25 = (f32[32,256]{1,0:T(8,128)S(1)}, f32[32,256]{1,0:T(8,128)S(1)}, u32[]{:S(2)}, u32[]{:S(2)}) collective-permute-start(f32[32,256]{1,0:T(8,128)S(1)} %fusion), channel_id=1, source_target_pairs={{0,10},{1,11},{2,12},{3,13},{4,14},{5,15},{6,16},{7,17},{8,18},{9,... | collective-permute-start | bytes 98312
  977.5 13.1 %collective-permute-start.26 = (f32[32,256]{1,0:T(8,128)S(1)}, f32[32,256]{1,0:T(8,128)S(1)}, u32[]{:S(2)}, u32[]{:S(2)}) collective-permute-start(f32[32,256]{1,0:T(8,128)S(1)} %fusion), channel_id=1, source_target_pairs={{0,11},{1,12},{2,13},{3,14},{4,15},{5,16},{6,17},{7,18},{8,19},{9,... | collective-permute-start | bytes 98312
  990.7 13.1 %collective-permute-start.27 = (f32[32,256]{1,0:T(8,128)S(1)}, f32[32,256]{1,0:T(8,128)S(1)}, u32[]{:S(2)}, u32[]{:S(2)}) collective-permute-start(f32[32,256]{1,0:T(8,128)S(1)} %fusion), channel_id=1, source_target_pairs={{0,12},{1,13},{2,14},{3,15},{4,16},{5,17},{6,18},{7,19},{8,20},{9,... | collective-permute-start | bytes 98312
  1003.8 13.1 %collective-permute-start.28 = (f32[32,256]{1,0:T(8,128)S(1)}, f32[32,256]{1,0:T(8,128)S(1)}, u32[]{:S(2)}, u32[]{:S(2)}) collective-permute-start(f32[32,256]{1,0:T(8,128)S(1)} %fusion), channel_id=1, source_target_pairs={{0,13},{1,14},{2,15},{3,16},{4,17},{5,18},{6,19},{7,20},{8,21},{9,... | collective-permute-start | bytes 98312
  1017.0 13.1 %collective-permute-start.29 = (f32[32,256]{1,0:T(8,128)S(1)}, f32[32,256]{1,0:T(8,128)S(1)}, u32[]{:S(2)}, u32[]{:S(2)}) collective-permute-start(f32[32,256]{1,0:T(8,128)S(1)} %fusion), channel_id=1, source_target_pairs={{0,14},{1,15},{2,16},{3,17},{4,18},{5,19},{6,20},{7,21},{8,22},{9,... | collective-permute-start | bytes 98312
  1030.1 13.1 %collective-permute-start.30 = (f32[32,256]{1,0:T(8,128)S(1)}, f32[32,256]{1,0:T(8,128)S(1)}, u32[]{:S(2)}, u32[]{:S(2)}) collective-permute-start(f32[32,256]{1,0:T(8,128)S(1)} %fusion), channel_id=1, source_target_pairs={{0,15},{1,16},{2,17},{3,18},{4,19},{5,20},{6,21},{7,22},{8,23},{9,... | collective-permute-start | bytes 98312
  1043.2 13.1 %collective-permute-start.31 = (f32[32,256]{1,0:T(8,128)S(1)}, f32[32,256]{1,0:T(8,128)S(1)}, u32[]{:S(2)}, u32[]{:S(2)}) collective-permute-start(f32[32,256]{1,0:T(8,128)S(1)} %fusion), channel_id=1, source_target_pairs={{0,16},{1,17},{2,18},{3,19},{4,20},{5,21},{6,22},{7,23},{8,24},{9,... | collective-permute-start | bytes 98312
  1056.4 13.1 %collective-permute-start.32 = (f32[32,256]{1,0:T(8,128)S(1)}, f32[32,256]{1,0:T(8,128)S(1)}, u32[]{:S(2)}, u32[]{:S(2)}) collective-permute-start(f32[32,256]{1,0:T(8,128)S(1)} %fusion), channel_id=1, source_target_pairs={{0,17},{1,18},{2,19},{3,20},{4,21},{5,22},{6,23},{7,24},{8,25},{9,... | collective-permute-start | bytes 98312
  1069.5 5.9 collective-permute-start.33
  1075.4 4.9 collective-permute-start.34
  1080.3 4.3 collective-permute-start.35
  1084.6 7.7 collective-permute-start.36
  1092.3 3.5 collective-permute-start.37
  1098.7 3.8 collective-permute-start.39
  1102.5 9.2 collective-permute-start.40
  1111.7 6.8 collective-permute-start.41
  1119.9 3.9 collective-permute-start.43
  1123.8 5.9 collective-permute-start.44
  1140.0 3.2 collective-permute-start.51
  1153.7 3.2 collective-permute-start.56
  1166.8 3.9 collective-permute-start.62
  1173.9 67.3 %concatenate.44 = f32[1562,256]{1,0:T(8,128)} concatenate(f32[26,256]{1,0:T(8,128)S(1)} %collective-permute-done.63, f32[32,256]{1,0:T(8,128)} %collective-permute-done.62, f32[32,256]{1,0:T(8,128)} %copy-done.41, f32[32,256]{1,0:T(8,128)} %copy-done.40, f32[32,256]{1,0:T(8,128)} %copy-done.39, f32[32,256]{1,0:T(8,128)} %copy-done.38, f32[32,256]{1,0:T(8,128)} %copy-done.37, ...), dimensions={0} | concatenate | bytes 3198976
  (234 shorter events, 79.8 us)
Async XLA Ops:
  65.2 24.0 %collective-permute-start.10 = (bf16[4,1,4,1,1,16,256]{6,5,2,0,4,3,1:T(8,128)(2,1)S(1)}, bf16[4,1,4,1,1,16,256]{6,5,2,0,4,3,1:T(8,128)(2,1)S(1)}, u32[]{:S(2)}, u32[]{:S(2)}) collective-permute-start(bf16[4,1,4,1,1,16,256]{6,5,2,0,4,3,1:T(8,128)(2,1)S(1)} %select_bitcast_fusion.5), channel_id=1, source_target_pairs={{0,1},{1,0},{2,3},{3,2},{4,5},{5,4},{6,7},{7,6},{8,9},{9,8},{10,11... | collective-permute-start | bytes 393224 | tf_op jit(solution)/shard_map/ppermute | solution.py:19
  67.7 24.5 %collective-permute-start.13 = (bf16[4,1,4,1,1,16,256]{6,5,2,0,4,3,1:T(8,128)(2,1)S(1)}, bf16[4,1,4,1,1,16,256]{6,5,2,0,4,3,1:T(8,128)(2,1)S(1)}, u32[]{:S(2)}, u32[]{:S(2)}) collective-permute-start(bf16[4,1,4,1,1,16,256]{6,5,2,0,4,3,1:T(8,128)(2,1)S(1)} %fusion.35), channel_id=1, source_target_pairs={{0,1},{1,0},{2,3},{3,2},{4,5},{5,4},{6,7},{7,6},{8,9},{9,8},{10,11... | collective-permute-start | bytes 393224 | tf_op jit(solution)/shard_map/ppermute | solution.py:19
  89.3 13.4 %collective-permute-start.11 = (bf16[4,1,2,2,1,16,256]{6,5,2,0,3,4,1:T(8,128)(2,1)S(1)}, bf16[4,1,2,2,1,16,256]{6,5,2,0,3,4,1:T(8,128)(2,1)S(1)}, u32[]{:S(2)}, u32[]{:S(2)}) collective-permute-start(bf16[4,1,2,2,1,16,256]{6,5,2,0,3,4,1:T(8,128)(2,1)S(1)} %select_bitcast_fusion.4), channel_id=1, source_target_pairs={{0,2},{2,0},{1,3},{3,1},{4,6},{6,4},{5,7},{7,5},{8,10},{10,8},{9,1... | collective-permute-start | bytes 393224 | tf_op jit(solution)/shard_map/ppermute | solution.py:19
  92.3 16.8 %collective-permute-start.14 = (bf16[4,1,2,2,1,16,256]{6,5,2,0,3,4,1:T(8,128)(2,1)S(1)}, bf16[4,1,2,2,1,16,256]{6,5,2,0,3,4,1:T(8,128)(2,1)S(1)}, u32[]{:S(2)}, u32[]{:S(2)}) collective-permute-start(bf16[4,1,2,2,1,16,256]{6,5,2,0,3,4,1:T(8,128)(2,1)S(1)} %fusion.36), channel_id=1, source_target_pairs={{0,2},{2,0},{1,3},{3,1},{4,6},{6,4},{5,7},{7,5},{8,10},{10,8},{9,1... | collective-permute-start | bytes 393224 | tf_op jit(solution)/shard_map/ppermute | solution.py:19
  102.8 17.5 %collective-permute-start.12 = (bf16[4,1,1,4,1,16,256]{6,5,3,0,4,2,1:T(8,128)(2,1)S(1)}, bf16[4,1,1,4,1,16,256]{6,5,3,0,4,2,1:T(8,128)(2,1)S(1)}, u32[]{:S(2)}, u32[]{:S(2)}) collective-permute-start(bf16[4,1,1,4,1,16,256]{6,5,3,0,4,2,1:T(8,128)(2,1)S(1)} %select_bitcast_fusion.3), channel_id=1, source_target_pairs={{0,4},{4,0},{1,5},{5,1},{2,6},{6,2},{3,7},{7,3},{8,12},{12,8},{9,1... | collective-permute-start | bytes 393224 | tf_op jit(solution)/shard_map/ppermute | solution.py:19
  110.0 15.5 %collective-permute-start.15 = (bf16[4,1,1,4,1,16,256]{6,5,3,0,4,2,1:T(8,128)(2,1)}, bf16[4,1,1,4,1,16,256]{6,5,3,0,4,2,1:T(8,128)(2,1)S(1)}, u32[]{:S(2)}, u32[]{:S(2)}) collective-permute-start(bf16[4,1,1,4,1,16,256]{6,5,3,0,4,2,1:T(8,128)(2,1)} %select_bitcast_fusion), channel_id=1, source_target_pairs={{0,4},{4,0},{1,5},{5,1},{2,6},{6,2},{3,7},{7,3},{8,12},{12,8},{9,1... | collective-permute-start | bytes 393224 | tf_op jit(solution)/shard_map/ppermute | solution.py:19
  830.6 81.3 %collective-permute-start.16 = (f32[32,256]{1,0:T(8,128)S(1)}, f32[32,256]{1,0:T(8,128)S(1)}, u32[]{:S(2)}, u32[]{:S(2)}) collective-permute-start(f32[32,256]{1,0:T(8,128)S(1)} %fusion), channel_id=1, source_target_pairs={{0,1},{1,2},{2,3},{3,4},{4,5},{5,6},{6,7},{7,8},{8,9},{9,10},{10,1... | collective-permute-start | bytes 98312
  856.0 69.0 %collective-permute-start.17 = (f32[32,256]{1,0:T(8,128)S(1)}, f32[32,256]{1,0:T(8,128)S(1)}, u32[]{:S(2)}, u32[]{:S(2)}) collective-permute-start(f32[32,256]{1,0:T(8,128)S(1)} %fusion), channel_id=1, source_target_pairs={{0,2},{1,3},{2,4},{3,5},{4,6},{5,7},{6,8},{7,9},{8,10},{9,11},{10,... | collective-permute-start | bytes 98312
  869.2 29.6 %collective-permute-start.63 = (f32[26,256]{1,0:T(8,128)S(1)}, f32[26,256]{1,0:T(8,128)S(1)}, u32[]{:S(2)}, u32[]{:S(2)}) collective-permute-start(f32[26,256]{1,0:T(8,128)S(1)} %slice.202), channel_id=1, source_target_pairs={{0,48},{1,49},{2,50},{3,51},{4,52},{5,53},{6,54},{7,55},{8,56},{9,... | collective-permute-start | bytes 79880
  874.9 63.2 %collective-permute-start.18 = (f32[32,256]{1,0:T(8,128)S(1)}, f32[32,256]{1,0:T(8,128)S(1)}, u32[]{:S(2)}, u32[]{:S(2)}) collective-permute-start(f32[32,256]{1,0:T(8,128)S(1)} %fusion), channel_id=1, source_target_pairs={{0,3},{1,4},{2,5},{3,6},{4,7},{5,8},{6,9},{7,10},{8,11},{9,12},{10... | collective-permute-start | bytes 98312
  885.6 65.7 %collective-permute-start.19 = (f32[32,256]{1,0:T(8,128)S(1)}, f32[32,256]{1,0:T(8,128)S(1)}, u32[]{:S(2)}, u32[]{:S(2)}) collective-permute-start(f32[32,256]{1,0:T(8,128)S(1)} %fusion), channel_id=1, source_target_pairs={{0,4},{1,5},{2,6},{3,7},{4,8},{5,9},{6,10},{7,11},{8,12},{9,13},{1... | collective-permute-start | bytes 98312
  898.7 65.7 %collective-permute-start.20 = (f32[32,256]{1,0:T(8,128)S(1)}, f32[32,256]{1,0:T(8,128)S(1)}, u32[]{:S(2)}, u32[]{:S(2)}) collective-permute-start(f32[32,256]{1,0:T(8,128)S(1)} %fusion), channel_id=1, source_target_pairs={{0,5},{1,6},{2,7},{3,8},{4,9},{5,10},{6,11},{7,12},{8,13},{9,14},{... | collective-permute-start | bytes 98312
  911.8 65.7 %collective-permute-start.21 = (f32[32,256]{1,0:T(8,128)S(1)}, f32[32,256]{1,0:T(8,128)S(1)}, u32[]{:S(2)}, u32[]{:S(2)}) collective-permute-start(f32[32,256]{1,0:T(8,128)S(1)} %fusion), channel_id=1, source_target_pairs={{0,6},{1,7},{2,8},{3,9},{4,10},{5,11},{6,12},{7,13},{8,14},{9,15},... | collective-permute-start | bytes 98312
  925.0 65.7 %collective-permute-start.22 = (f32[32,256]{1,0:T(8,128)S(1)}, f32[32,256]{1,0:T(8,128)S(1)}, u32[]{:S(2)}, u32[]{:S(2)}) collective-permute-start(f32[32,256]{1,0:T(8,128)S(1)} %fusion), channel_id=1, source_target_pairs={{0,7},{1,8},{2,9},{3,10},{4,11},{5,12},{6,13},{7,14},{8,15},{9,16}... | collective-permute-start | bytes 98312
  938.1 65.7 %collective-permute-start.23 = (f32[32,256]{1,0:T(8,128)S(1)}, f32[32,256]{1,0:T(8,128)S(1)}, u32[]{:S(2)}, u32[]{:S(2)}) collective-permute-start(f32[32,256]{1,0:T(8,128)S(1)} %fusion), channel_id=1, source_target_pairs={{0,8},{1,9},{2,10},{3,11},{4,12},{5,13},{6,14},{7,15},{8,16},{9,17... | collective-permute-start | bytes 98312
  951.3 65.7 %collective-permute-start.24 = (f32[32,256]{1,0:T(8,128)S(1)}, f32[32,256]{1,0:T(8,128)S(1)}, u32[]{:S(2)}, u32[]{:S(2)}) collective-permute-start(f32[32,256]{1,0:T(8,128)S(1)} %fusion), channel_id=1, source_target_pairs={{0,9},{1,10},{2,11},{3,12},{4,13},{5,14},{6,15},{7,16},{8,17},{9,1... | collective-permute-start | bytes 98312
  964.4 65.7 %collective-permute-start.25 = (f32[32,256]{1,0:T(8,128)S(1)}, f32[32,256]{1,0:T(8,128)S(1)}, u32[]{:S(2)}, u32[]{:S(2)}) collective-permute-start(f32[32,256]{1,0:T(8,128)S(1)} %fusion), channel_id=1, source_target_pairs={{0,10},{1,11},{2,12},{3,13},{4,14},{5,15},{6,16},{7,17},{8,18},{9,... | collective-permute-start | bytes 98312
  977.5 65.7 %collective-permute-start.26 = (f32[32,256]{1,0:T(8,128)S(1)}, f32[32,256]{1,0:T(8,128)S(1)}, u32[]{:S(2)}, u32[]{:S(2)}) collective-permute-start(f32[32,256]{1,0:T(8,128)S(1)} %fusion), channel_id=1, source_target_pairs={{0,11},{1,12},{2,13},{3,14},{4,15},{5,16},{6,17},{7,18},{8,19},{9,... | collective-permute-start | bytes 98312
  990.7 65.7 %collective-permute-start.27 = (f32[32,256]{1,0:T(8,128)S(1)}, f32[32,256]{1,0:T(8,128)S(1)}, u32[]{:S(2)}, u32[]{:S(2)}) collective-permute-start(f32[32,256]{1,0:T(8,128)S(1)} %fusion), channel_id=1, source_target_pairs={{0,12},{1,13},{2,14},{3,15},{4,16},{5,17},{6,18},{7,19},{8,20},{9,... | collective-permute-start | bytes 98312
  1003.8 65.7 %collective-permute-start.28 = (f32[32,256]{1,0:T(8,128)S(1)}, f32[32,256]{1,0:T(8,128)S(1)}, u32[]{:S(2)}, u32[]{:S(2)}) collective-permute-start(f32[32,256]{1,0:T(8,128)S(1)} %fusion), channel_id=1, source_target_pairs={{0,13},{1,14},{2,15},{3,16},{4,17},{5,18},{6,19},{7,20},{8,21},{9,... | collective-permute-start | bytes 98312
  1017.0 58.4 %collective-permute-start.29 = (f32[32,256]{1,0:T(8,128)S(1)}, f32[32,256]{1,0:T(8,128)S(1)}, u32[]{:S(2)}, u32[]{:S(2)}) collective-permute-start(f32[32,256]{1,0:T(8,128)S(1)} %fusion), channel_id=1, source_target_pairs={{0,14},{1,15},{2,16},{3,17},{4,18},{5,19},{6,20},{7,21},{8,22},{9,... | collective-permute-start | bytes 98312
  1030.1 50.2 %collective-permute-start.30 = (f32[32,256]{1,0:T(8,128)S(1)}, f32[32,256]{1,0:T(8,128)S(1)}, u32[]{:S(2)}, u32[]{:S(2)}) collective-permute-start(f32[32,256]{1,0:T(8,128)S(1)} %fusion), channel_id=1, source_target_pairs={{0,15},{1,16},{2,17},{3,18},{4,19},{5,20},{6,21},{7,22},{8,23},{9,... | collective-permute-start | bytes 98312
  1043.2 41.4 %collective-permute-start.31 = (f32[32,256]{1,0:T(8,128)S(1)}, f32[32,256]{1,0:T(8,128)S(1)}, u32[]{:S(2)}, u32[]{:S(2)}) collective-permute-start(f32[32,256]{1,0:T(8,128)S(1)} %fusion), channel_id=1, source_target_pairs={{0,16},{1,17},{2,18},{3,19},{4,20},{5,21},{6,22},{7,23},{8,24},{9,... | collective-permute-start | bytes 98312
  1056.4 35.9 %collective-permute-start.32 = (f32[32,256]{1,0:T(8,128)S(1)}, f32[32,256]{1,0:T(8,128)S(1)}, u32[]{:S(2)}, u32[]{:S(2)}) collective-permute-start(f32[32,256]{1,0:T(8,128)S(1)} %fusion), channel_id=1, source_target_pairs={{0,17},{1,18},{2,19},{3,20},{4,21},{5,22},{6,23},{7,24},{8,25},{9,... | collective-permute-start | bytes 98312
  1069.5 26.3 %collective-permute-start.33 = (f32[32,256]{1,0:T(8,128)S(1)}, f32[32,256]{1,0:T(8,128)S(1)}, u32[]{:S(2)}, u32[]{:S(2)}) collective-permute-start(f32[32,256]{1,0:T(8,128)S(1)} %fusion), channel_id=1, source_target_pairs={{0,18},{1,19},{2,20},{3,21},{4,22},{5,23},{6,24},{7,25},{8,26},{9,... | collective-permute-start | bytes 98312
  1075.4 23.2 %collective-permute-start.34 = (f32[32,256]{1,0:T(8,128)S(1)}, f32[32,256]{1,0:T(8,128)S(1)}, u32[]{:S(2)}, u32[]{:S(2)}) collective-permute-start(f32[32,256]{1,0:T(8,128)S(1)} %fusion), channel_id=1, source_target_pairs={{0,19},{1,20},{2,21},{3,22},{4,23},{5,24},{6,25},{7,26},{8,27},{9,... | collective-permute-start | bytes 98312
  1080.3 22.2 %collective-permute-start.35 = (f32[32,256]{1,0:T(8,128)S(1)}, f32[32,256]{1,0:T(8,128)S(1)}, u32[]{:S(2)}, u32[]{:S(2)}) collective-permute-start(f32[32,256]{1,0:T(8,128)S(1)} %fusion), channel_id=1, source_target_pairs={{0,20},{1,21},{2,22},{3,23},{4,24},{5,25},{6,26},{7,27},{8,28},{9,... | collective-permute-start | bytes 98312
  1084.6 27.1 %collective-permute-start.36 = (f32[32,256]{1,0:T(8,128)S(1)}, f32[32,256]{1,0:T(8,128)S(1)}, u32[]{:S(2)}, u32[]{:S(2)}) collective-permute-start(f32[32,256]{1,0:T(8,128)S(1)} %fusion), channel_id=1, source_target_pairs={{0,21},{1,22},{2,23},{3,24},{4,25},{5,26},{6,27},{7,28},{8,29},{9,... | collective-permute-start | bytes 98312
  1092.3 26.2 %collective-permute-start.37 = (f32[32,256]{1,0:T(8,128)S(1)}, f32[32,256]{1,0:T(8,128)S(1)}, u32[]{:S(2)}, u32[]{:S(2)}) collective-permute-start(f32[32,256]{1,0:T(8,128)S(1)} %fusion), channel_id=1, source_target_pairs={{0,22},{1,23},{2,24},{3,25},{4,26},{5,27},{6,28},{7,29},{8,30},{9,... | collective-permute-start | bytes 98312
  1095.8 24.1 %collective-permute-start.38 = (f32[32,256]{1,0:T(8,128)S(1)}, f32[32,256]{1,0:T(8,128)S(1)}, u32[]{:S(2)}, u32[]{:S(2)}) collective-permute-start(f32[32,256]{1,0:T(8,128)S(1)} %fusion), channel_id=1, source_target_pairs={{0,23},{1,24},{2,25},{3,26},{4,27},{5,28},{6,29},{7,30},{8,31},{9,... | collective-permute-start | bytes 98312
  1098.7 25.1 %collective-permute-start.39 = (f32[32,256]{1,0:T(8,128)S(1)}, f32[32,256]{1,0:T(8,128)S(1)}, u32[]{:S(2)}, u32[]{:S(2)}) collective-permute-start(f32[32,256]{1,0:T(8,128)S(1)} %fusion), channel_id=1, source_target_pairs={{0,24},{1,25},{2,26},{3,27},{4,28},{5,29},{6,30},{7,31},{8,32},{9,... | collective-permute-start | bytes 98312
  1102.5 27.2 %collective-permute-start.40 = (f32[32,256]{1,0:T(8,128)S(1)}, f32[32,256]{1,0:T(8,128)S(1)}, u32[]{:S(2)}, u32[]{:S(2)}) collective-permute-start(f32[32,256]{1,0:T(8,128)S(1)} %fusion), channel_id=1, source_target_pairs={{0,25},{1,26},{2,27},{3,28},{4,29},{5,30},{6,31},{7,32},{8,33},{9,... | collective-permute-start | bytes 98312
  1111.7 19.9 %collective-permute-start.41 = (f32[32,256]{1,0:T(8,128)S(1)}, f32[32,256]{1,0:T(8,128)S(1)}, u32[]{:S(2)}, u32[]{:S(2)}) collective-permute-start(f32[32,256]{1,0:T(8,128)S(1)} %fusion), channel_id=1, source_target_pairs={{0,26},{1,27},{2,28},{3,29},{4,30},{5,31},{6,32},{7,33},{8,34},{9,... | collective-permute-start | bytes 98312
  1118.6 14.9 %collective-permute-start.42 = (f32[32,256]{1,0:T(8,128)S(1)}, f32[32,256]{1,0:T(8,128)S(1)}, u32[]{:S(2)}, u32[]{:S(2)}) collective-permute-start(f32[32,256]{1,0:T(8,128)S(1)} %fusion), channel_id=1, source_target_pairs={{0,27},{1,28},{2,29},{3,30},{4,31},{5,32},{6,33},{7,34},{8,35},{9,... | collective-permute-start | bytes 98312
  1119.9 15.5 %collective-permute-start.43 = (f32[32,256]{1,0:T(8,128)S(1)}, f32[32,256]{1,0:T(8,128)}, u32[]{:S(2)}, u32[]{:S(2)}) collective-permute-start(f32[32,256]{1,0:T(8,128)S(1)} %fusion), channel_id=1, source_target_pairs={{0,28},{1,29},{2,30},{3,31},{4,32},{5,33},{6,34},{7,35},{8,36},{9,... | collective-permute-start | bytes 98312
  1123.8 12.9 %collective-permute-start.44 = (f32[32,256]{1,0:T(8,128)S(1)}, f32[32,256]{1,0:T(8,128)}, u32[]{:S(2)}, u32[]{:S(2)}) collective-permute-start(f32[32,256]{1,0:T(8,128)S(1)} %fusion), channel_id=1, source_target_pairs={{0,29},{1,30},{2,31},{3,32},{4,33},{5,34},{6,35},{7,36},{8,37},{9,... | collective-permute-start | bytes 98312
  1135.4 12.3 collective-permute-start.48
  1136.7 12.6 %collective-permute-start.49 = (f32[32,256]{1,0:T(8,128)S(1)}, f32[32,256]{1,0:T(8,128)S(1)}, u32[]{:S(2)}, u32[]{:S(2)}) collective-permute-start(f32[32,256]{1,0:T(8,128)S(1)} %fusion), channel_id=1, source_target_pairs={{0,34},{1,35},{2,36},{3,37},{4,38},{5,39},{6,40},{7,41},{8,42},{9,... | collective-permute-start | bytes 98312
  1138.7 13.3 %collective-permute-start.50 = (f32[32,256]{1,0:T(8,128)S(1)}, f32[32,256]{1,0:T(8,128)S(1)}, u32[]{:S(2)}, u32[]{:S(2)}) collective-permute-start(f32[32,256]{1,0:T(8,128)S(1)} %fusion), channel_id=1, source_target_pairs={{0,35},{1,36},{2,37},{3,38},{4,39},{5,40},{6,41},{7,42},{8,43},{9,... | collective-permute-start | bytes 98312
  1140.0 13.6 %collective-permute-start.51 = (f32[32,256]{1,0:T(8,128)S(1)}, f32[32,256]{1,0:T(8,128)S(1)}, u32[]{:S(2)}, u32[]{:S(2)}) collective-permute-start(f32[32,256]{1,0:T(8,128)S(1)} %fusion), channel_id=1, source_target_pairs={{0,36},{1,37},{2,38},{3,39},{4,40},{5,41},{6,42},{7,43},{8,44},{9,... | collective-permute-start | bytes 98312
  1143.3 13.6 %collective-permute-start.52 = (f32[32,256]{1,0:T(8,128)S(1)}, f32[32,256]{1,0:T(8,128)S(1)}, u32[]{:S(2)}, u32[]{:S(2)}) collective-permute-start(f32[32,256]{1,0:T(8,128)S(1)} %fusion), channel_id=1, source_target_pairs={{0,37},{1,38},{2,39},{3,40},{4,41},{5,42},{6,43},{7,44},{8,45},{9,... | collective-permute-start | bytes 98312
  1147.7 12.0 collective-permute-start.53
  1149.4 11.6 collective-permute-start.54
  1152.0 10.4 collective-permute-start.55
  1153.7 11.4 collective-permute-start.56
  1159.7 12.8 %collective-permute-start.58 = (f32[32,256]{1,0:T(8,128)S(1)}, f32[32,256]{1,0:T(8,128)S(1)}, u32[]{:S(2)}, u32[]{:S(2)}) collective-permute-start(f32[32,256]{1,0:T(8,128)S(1)} %fusion), channel_id=1, source_target_pairs={{0,43},{1,44},{2,45},{3,46},{4,47},{5,48},{6,49},{7,50},{8,51},{9,... | collective-permute-start | bytes 98312
  1161.0 11.5 collective-permute-start.59
  1162.4 10.1 collective-permute-start.60
  (60 other events, 2571.4 us)
where the time goes:
time: 1250 us; the launch traced here: 1240 us
  blocking collectives  695 us (56%)
  starting transfers between devices  407 us (33%)
  local copies, waits for them, and re-layouts  96.6 us (8%)
  other arithmetic  16 us (1%)
  waiting for transfers between devices  14.1 us (1%)
    unnamed x1, blocking collectives  695 us
    unnamed x48, starting transfers between devices  336 us
    unnamed x98, local copies, waits for them, and re-layouts  73.4 us
    ppermute x12, starting transfers between devices, from_partner(): return lax.ppermute(block, axis, route)  58.2 us
  transfers between devices with their start and end apart: 64, of which 8 were waited for; matrix products, arithmetic and copies ran while one was open for 1% of the time, Pallas kernels for 0%

commit v1 on v0

v1 whole, which is shorter than its diff:
```python
import math

import jax
import jax.numpy as jnp
import ml_dtypes
import numpy as np
from jax import lax
from jax.experimental import pallas as pl
from jax.experimental.pallas import tpu as pltpu
from jax.sharding import PartitionSpec as P

MESH = pl.DeviceIdType.MESH
BF = jnp.bfloat16
F32 = jnp.float32

DIRS = ((-1, 0), (1, 0), (0, -1), (0, 1), (-1, -1), (-1, 1), (1, -1), (1, 1))
MAIN = (32, 32, 16, 16, 0, 0, 0, 0)
SIZE = tuple(4 * m + 16 for m in MAIN)
START = tuple(sum(SIZE[:d]) for d in range(8))
MAIN_AT = (0, 32, 64, 80)

CHUNK = 416
HEAD_ROWS = 26


def weight(cell, fine, cells, first, last):
    at = fine - 2 * cell
    value = 0.75 if at in (0, 1) else 0.25 if at in (-1, 2) else 0.0
    if first and cell == 0 and fine == 0:
        value += 0.25
    if last and cell == cells - 1 and fine == 2 * cells - 1:
        value += 0.25
    return value


def halo_cells(d):
    dr, dc = DIRS[d]
    rows = {1: [-1, 0], -1: [8, 7], 0: list(range(8))}[dr]
    cols = {1: [-1, 0], -1: [16, 15], 0: list(range(16))}[dc]
    if dr and dc:
        return [], [(j, w) for j in rows for w in cols]
    main = [(j, w) for j in rows for w in cols]
    if dr:
        corner = [(j, w) for j in rows for w in (-1, 16)]
    else:
        corner = [(j, w) for j in (-1, 8) for w in cols]
    return main, corner


def tables():
    send = np.zeros((9, 128, 512), np.float32)
    take = np.zeros((9, 480, 640), np.float32)
    for place in range(9):
        top, bottom = place // 3 == 0, place // 3 == 2
        left, right = place % 3 == 0, place % 3 == 2
        row_w = np.array([[weight(j, r, 8, top, bottom) for r in range(16)] for j in range(-1, 9)])
        col_w = np.array([[weight(w, c, 16, left, right) for c in range(32)] for w in range(-1, 17)])

        def line(j, w):
            return np.outer(row_w[j + 1], col_w[w + 1]).reshape(512)

        for d, (dr, dc) in enumerate(DIRS):
            main, corner = halo_cells(d)
            for m, (j, w) in enumerate(main):
                send[place, MAIN_AT[d] + m] = line(j + 8 * dr, w + 16 * dc)
            for m, (j, w) in enumerate(corner):
                send[place, 96 + 4 * d + m] = line(j + 8 * dr, w + 16 * dc)

        def outside(j, w):
            return (j < 0 and top) or (j > 7 and bottom) or (w < 0 and left) or (w > 15 and right)

        for shift in range(3):
            for jr in range(10):
                for ww in range(16):
                    j, w = jr - 1, shift + ww - 1
                    if not outside(j, w):
                        take[place, shift * 160 + jr * 16 + ww, :512] = line(j, w)
            for d in range(8):
                main, corner = halo_cells(d)
                at = [(512 + MAIN_AT[d] + m, cell) for m, cell in enumerate(main)] if main else []
                at += [(608 + 4 * d + m, cell) for m, cell in enumerate(corner)]
                for column, (j, w) in at:
                    ww = w + 1 - shift
                    if 0 <= ww < 16 and not outside(j, w):
                        take[place, shift * 160 + (j + 1) * 16 + ww, column] = 1.0
    order = np.zeros((128, 128), np.float32)
    for i in range(4):
        for d in range(8):
            for cell in range(4):
                order[d * 16 + i * 4 + cell, i * 32 + d * 4 + cell] = 1.0
    as_bf16 = [a.astype(ml_dtypes.bfloat16) for a in (send, take, np.stack([order, order.T]))]
    return as_bf16


def mm(a, b):
    return jnp.dot(a, b, preferred_element_type=F32)


def mm_t(a, b):
    return lax.dot_general(a, b, (((1,), (1,)), ((), ())), preferred_element_type=F32)


def kernel(
    cot_hbm, saved_hbm, feat_hbm, w_hbm, send_hbm, take_hbm, order_hbm,
    tok_out, head_out,
    cot, saved, feat, wconv, send_m, take_m, order_m,
    saved_t, feat_t, halo_out, halo_in, corner, acc, pooled, grad_acc, grad, tok,
    head, send_c, recv_c, part, send_1, recv_1, send_2, recv_2, last, send_3, recv_3,
    load_sem, halo_ss, halo_rs, tok_ss, tok_rs, c_ss, c_rs, ss_1, rs_1, ss_2, rs_2, ss_3, rs_3, out_sem,
):
    dp = lax.axis_index("dp")
    tile = lax.axis_index("tile")
    z, y, xh, core = tile // 16, (tile // 4) % 4, (tile // 2) % 2, tile % 2
    x = xh * 2 + dp
    g, row = tile % 8, tile // 8
    g0, g1, g2 = g % 2, (g // 2) % 2, g // 4
    col = g2 * 4 + (g2 + g1) % 2 * 2 + (g2 + g1 + g0) % 2
    a = jnp.where(core == 0, x, y)
    b = jnp.where(core == 0, y, x)

    def gray(c):
        c0, c1, c2 = c % 2, (c // 2) % 2, c // 4
        return c2 * 4 + (c2 + c1) % 2 * 2 + (c1 + c0) % 2

    def in_plane(to_a, to_b):
        to_x = jnp.where(core == 0, to_a, to_b)
        to_y = jnp.where(core == 0, to_b, to_a)
        return {"dp": to_x % 2, "tile": z * 16 + to_y * 4 + to_x // 2 * 2 + core}

    def remote(src, dst, send_sem, recv_sem, device):
        return pltpu.make_async_remote_copy(
            src_ref=src, dst_ref=dst, send_sem=send_sem, recv_sem=recv_sem,
            device_id=device, device_id_type=MESH,
        )

    place = (
        jnp.where(row == 0, 0, jnp.where(row == 15, 2, 1)) * 3
        + jnp.where(col == 0, 0, jnp.where(col == 7, 2, 1))
    )
    loads = [
        pltpu.make_async_copy(src, dst, load_sem.at[n])
        for n, (src, dst) in enumerate([
            (cot_hbm, cot), (send_hbm.at[place], send_m), (order_hbm, order_m),
            (take_hbm.at[place], take_m), (saved_hbm, saved), (w_hbm, wconv), (feat_hbm, feat),
        ])
    ]
    for load in loads:
        load.start()

    for n in range(3):
        loads[n].wait()
    for i in range(4):
        r = mm(send_m[...], cot[i]).astype(BF)
        for d in range(4):
            m = MAIN[d]
            halo_out[START[d] + i * m : START[d] + (i + 1) * m, :] = r[MAIN_AT[d] : MAIN_AT[d] + m]
        corner[i * 32 : (i + 1) * 32, :] = r[96:128]
    corners = mm(order_m[0], corner[...]).astype(BF)
    for d in range(8):
        halo_out[START[d] + 4 * MAIN[d] : START[d] + SIZE[d], :] = corners[d * 16 : d * 16 + 16]

    def halo(d):
        dr, dc = DIRS[d]
        there = jnp.clip(row + dr, 0, 15) * 8 + gray(jnp.clip(col + dc, 0, 7))
        return remote(
            halo_out.at[START[d] : START[d] + SIZE[d]], halo_in.at[START[d] : START[d] + SIZE[d]],
            halo_ss.at[d], halo_rs.at[d], {"tile": there},
        )

    def has(dr, dc):
        to_row, to_col = row + dr, col + dc
        ok = jnp.logical_and(to_row >= 0, to_row < 16)
        return jnp.logical_and(ok, jnp.logical_and(to_col >= 0, to_col < 8))

    for d in range(8):
        dr, dc = DIRS[d]

        @pl.when(has(dr, dc))
        def _():
            halo(d).start()

        @pl.when(jnp.logical_not(has(-dr, -dc)))
        def _():
            halo_in[START[d] : START[d] + SIZE[d], :] = jnp.zeros((SIZE[d], 256), BF)

    loads[3].wait()
    for i in range(4):
        acc[i] = mm(take_m[:, :512], cot[i])
    loads[4].wait()
    for k in range(2):
        for i in range(4):
            saved_t[k * 256 : (k + 1) * 256, i * 128 : (i + 1) * 128] = saved[i, k].T

    for d in range(8):
        dr, dc = DIRS[d]

        @pl.when(has(-dr, -dc))
        def _():
            halo(d).wait_recv()

    for d in range(8):
        at = START[d] + 4 * MAIN[d]
        corner[d * 16 : d * 16 + 16, :] = halo_in[at : at + 16, :]
    corners = mm(order_m[1], corner[...]).astype(BF)
    for i in range(4):
        parts = [halo_in[START[d] + i * MAIN[d] : START[d] + (i + 1) * MAIN[d], :] for d in range(4)]
        ring = jnp.concatenate(parts + [corners[i * 32 : (i + 1) * 32]], axis=0)
        full = (acc[i] + mm(take_m[:, 512:], ring)).astype(BF)
        for shift in range(3):
            pooled[shift, i] = full[shift * 160 : (shift + 1) * 160]

    def tap(t):
        u, v = t // 3, t % 3
        return pooled[2 - v, :, (2 - u) * 16 : (2 - u) * 16 + 128, :].reshape(512, 256)

    loads[5].wait()
    for k in range(2):
        for t in range(9):
            term = mm_t(tap(t), wconv[k * 9 + t])
            if t == 0:
                grad_acc[...] = term
            elif t < 8:
                grad_acc[...] += term
            else:
                grad[k] = (grad_acc[...] + term).astype(BF).reshape(4, 128, 256)

    def regroup(n):
        there = (g + n) % 8
        return remote(
            grad.at[:, :, pl.ds(pl.multiple_of(there * 16, 16), 16)],
            tok.at[:, :, pl.ds(pl.multiple_of(col * 16, 16), 16)],
            tok_ss.at[n], tok_rs.at[n], {"tile": row * 8 + there},
        )

    for n in range(1, 8):
        regroup(n).start()
    tok[:, :, pl.ds(pl.multiple_of(col * 16, 16), 16)] = grad[:, :, pl.ds(pl.multiple_of(g * 16, 16), 16)]

    mine = pl.ds(pl.multiple_of(core * 128, 128), 128)
    theirs = pl.ds(pl.multiple_of((1 - core) * 128, 128), 128)
    pair = {"tile": tile + 1 - 2 * core}

    def swap(q):
        return remote(send_c.at[q], recv_c.at[q], c_ss.at[q], c_rs.at[q], pair)

    def first(q, to_a):
        slot = (to_a - a + 4) % 4
        return remote(
            send_1.at[q], recv_1.at[q // 4, slot - 1], ss_1.at[q], rs_1.at[q // 4, slot - 1], in_plane(to_a, b)
        )

    def ready(q):
        send_c[q] = head[q * CHUNK : (q + 1) * CHUNK, theirs].astype(BF)
        swap(q).start()

    def reduced(q):
        swap(q).wait_recv()
        total = head[q * CHUNK : (q + 1) * CHUNK, mine] + recv_c[q].astype(F32)
        part[q] = total
        send_1[q] = total.astype(BF)

        @pl.when(a != q % 4)
        def _():
            first(q, q % 4).start()

    for k in range(2):
        for t in range(9):
            at = 2048 + (k * 9 + t) * 256
            head[at : at + 256, :] = mm(saved_t[k * 256 : (k + 1) * 256, :], tap(t))
        for q in (range(5, 10), range(10, 16))[k]:
            ready(q)
    loads[6].wait()
    for k in range(2):
        for i in range(4):
            feat_t[k * 1024 : (k + 1) * 1024, i * 128 : (i + 1) * 128] = feat[i, k].T
    for q in range(5, 16):
        reduced(q)

    for n in range(1, 8):
        regroup(n).wait_recv()
    out_copy = pltpu.make_async_copy(tok, tok_out, out_sem)
    out_copy.start()
    for k in range(2):
        for h in range(4):
            at = k * 1024 + h * 256
            head[at : at + 256, :] = mm(feat_t[at : at + 256, :], tok[k].reshape(512, 256))
        for q in (range(0, 2), range(2, 5))[k]:
            ready(q)
    for q in range(0, 5):
        reduced(q)

    def second(to_b):
        slot = (to_b - b + 4) % 4
        return remote(
            send_2.at[to_b], recv_2.at[slot - 1], ss_2.at[slot - 1], rs_2.at[slot - 1], in_plane(a, to_b)
        )

    for j in (3, 2, 1, 0):
        total = part[j * 4 + a]
        for s in range(3):
            first(j * 4 + 0, (a + s + 1) % 4).wait_recv()
            total = total + recv_1[j, s].astype(F32)
        part[j * 4 + a] = total
        send_2[j] = total.astype(BF)

        @pl.when(b != j)
        def _():
            second(j).start()

    total = part[b * 4 + a]
    for s in range(3):
        second((b + s + 1) % 4).wait_recv()
        total = total + recv_2[s].astype(F32)
    last[0:CHUNK, :] = total
    last[CHUNK:432, :] = jnp.zeros((16, 128), F32)
    for p in range(16):
        send_3[p] = last[p * HEAD_ROWS : p * HEAD_ROWS + 32, :].astype(BF)

    held = b * 4 + a
    own = dp * 8 + z

    def third(p):
        return remote(
            send_3.at[p], recv_3.at[z, core], ss_3.at[p], rs_3.at[z, core],
            {"dp": held // 8, "tile": held % 8 * 16 + p},
        )

    def to_self(p):
        return jnp.logical_and(held == own, tile % 16 == p)

    for p in range(16):

        @pl.when(jnp.logical_not(to_self(p)))
        def _():
            third(p).start()

        @pl.when(to_self(p))
        def _():
            recv_3[z, core] = send_3[p]

    total = [None, None]
    for cc in range(2):
        from_x = own % 4 if cc == 0 else own // 4
        from_y = own // 4 if cc == 0 else own % 4
        for zz in range(8):
            source = zz * 16 + from_y * 4 + from_x // 2 * 2 + cc
            itself = jnp.logical_and(from_x % 2 == dp, source == tile)

            @pl.when(jnp.logical_not(itself))
            def _():
                remote(
                    send_3.at[0], recv_3.at[zz, cc], ss_3.at[0], rs_3.at[zz, cc],
                    {"dp": from_x % 2, "tile": source},
                ).wait_recv()

            piece = recv_3[zz, cc].astype(F32)
            total[cc] = piece if zz == 0 else total[cc] + piece
    scale = 1.0 / math.sqrt(8 * 16384)
    for cc in range(2):
        head_out[:, cc * 128 : (cc + 1) * 128] = total[cc][:HEAD_ROWS] * scale

    for d in range(8):

        @pl.when(has(*DIRS[d]))
        def _():
            halo(d).wait_send()

    for n in range(1, 8):
        regroup(n).wait_send()
    for q in range(16):
        swap(q).wait_send()

        @pl.when(a != q % 4)
        def _():
            first(q, q % 4).wait_send()

    for s in range(3):
        second((b + s + 1) % 4).wait_send()
    for p in range(16):

        @pl.when(jnp.logical_not(to_self(p)))
        def _():
            third(p).wait_send()

    out_copy.wait()


def per_device(features, proj_weight, conv_weight, saved, cotangent):
    send, take, order = (jnp.asarray(t) for t in tables())
    hbm = pl.BlockSpec(memory_space=pl.ANY)
    dma = pltpu.SemaphoreType.DMA
    vmem = pltpu.VMEM
    tok, head = pl.pallas_call(
        kernel,
        out_shape=(
            jax.ShapeDtypeStruct((2, 4, 128, 256), BF),
            jax.ShapeDtypeStruct((HEAD_ROWS, 256), F32),
        ),
        in_specs=[hbm] * 7,
        out_specs=(hbm, pl.BlockSpec(memory_space=pltpu.VMEM)),
        scratch_shapes=[
            vmem((4, 512, 256), BF), vmem((4, 2, 128, 256), BF), vmem((4, 2, 128, 1024), BF),
            vmem((18, 256, 256), BF), vmem((128, 512), BF), vmem((480, 640), BF), vmem((2, 128, 128), BF),
            vmem((512, 512), BF), vmem((2048, 512), BF), vmem((512, 256), BF), vmem((512, 256), BF),
            vmem((128, 256), BF), vmem((4, 480, 256), F32), vmem((3, 4, 160, 256), BF),
            vmem((512, 256), F32), vmem((2, 4, 128, 256), BF), vmem((2, 4, 128, 256), BF),
            vmem((6656, 256), F32), vmem((16, CHUNK, 128), BF), vmem((16, CHUNK, 128), BF),
            vmem((16, CHUNK, 128), F32), vmem((16, CHUNK, 128), BF), vmem((4, 3, CHUNK, 128), BF),
            vmem((4, CHUNK, 128), BF), vmem((3, CHUNK, 128), BF), vmem((432, 128), F32),
            vmem((16, 32, 128), BF), vmem((8, 2, 32, 128), BF),
            dma((7,)), dma((8,)), dma((8,)), dma((8,)), dma((8,)), dma((16,)), dma((16,)),
            dma((16,)), dma((4, 3)), dma((3,)), dma((3,)), dma((16,)), dma((8, 2)), dma,
        ],
        compiler_params=pltpu.CompilerParams(has_side_effects=True, vmem_limit_bytes=56 * 2**20),
        cost_estimate=pl.CostEstimate(flops=3_000_000_000, bytes_accessed=9_000_000, transcendentals=0),
        name="head_backward",
    )(
        cotangent.reshape(4, 512, 256),
        saved.reshape(4, 2, 128, 256),
        features,
        conv_weight.reshape(18, 256, 256),
        send,
        take,
        order,
    )
    feature_grad = jnp.einsum("kinc,kdc->iknd", tok, proj_weight, preferred_element_type=F32)
    return feature_grad.astype(BF), head


def solution(mesh):
    in_specs = (
        P("dp", None, "tile", None),
        P(),
        P(),
        P("dp", None, "tile", None, None),
        P("dp", "tile", None, None),
    )
    out_specs = (P("dp", None, "tile", None), P(("dp", "tile"), None))
    return jax.shard_map(
        per_device, mesh=mesh, in_specs=in_specs, out_specs=out_specs, check_vma=False
    )
```

time: 1250 us -> 70.5 us (0.06)
  blocking collectives: 695 us -> 0 us
  starting transfers between devices: 407 us -> 0 us
  local copies, waits for them, and re-layouts: 96.6 us -> 2.12 us
  Pallas kernels: 0 us -> 65.2 us
  other arithmetic: 16 us -> 0 us
  waiting for transfers between devices: 14.1 us -> 0 us
    unnamed x1 -> x0, blocking collectives: 695 us -> none
    unnamed x48 -> x0, starting transfers between devices: 336 us -> none
    ppermute x16 -> x0, starting transfers between devices: 71.4 us -> none  [the longest x12 58.2 us: from_partner(): return lax.ppermute(block, axis, route)]
    unnamed x98 -> x6, local copies, waits for them, and re-layouts: 73.4 us -> 2.12 us
    pallas_call x0 -> x1, Pallas kernels: none -> 65.2 us  [per_device(): pl.pallas_call(kernel, out_shape=(jax.ShapeDtypeStruct((2, 4, 128, 256),...]
    slice x5 -> x0, local copies, waits for them, and re-layouts: 19.2 us -> none  [the longest x1 5.13 us: pool(): odd_part = lax.slice_in_dim(values_in, 2, 2 * cell_count + 2, 2, along_dim)]
    ppermute x16 -> x0, waiting for transfers between devices: 13.9 us -> none  [the longest x12 7.53 us: from_partner(): return lax.ppermute(block, axis, route)]
  transfers between devices with their start and end apart: 64 -> 0, of which waited for: 8 -> 0; matrix products, arithmetic and copies ran while one was open for 1% -> 0% of each run, Pallas kernels for 0% -> 0%
where the time goes in v1:
time: 70.5 us; the launch traced here: 69.8 us
  Pallas kernels  65.2 us (92%)
  local copies, waits for them, and re-layouts  2.12 us (3%)
  matrix products  1.78 us (3%)
    pallas_call x1, Pallas kernels, per_device(): pl.pallas_call(kernel, out_shape=(jax.ShapeDtypeStruct((2, 4, 128, 256),...  65.2 us
    unnamed x6, local copies, waits for them, and re-layouts  2.12 us
    dot_general x1, matrix products, per_device(): jnp.einsum('kinc,kdc->iknd', tok, proj_weight, preferred_element_type=F32)  1.78 us

profile of v1, /device:TPU:1, one launch (start us, length us, event | category | flops | bytes accessed | tf_op | source)
XLA Modules:
  0.0 69.8 jit_solution(12166072726531065463)
XLA Ops:
  0.6 0.0 copy-start
  0.6 65.2 %head_backward.1 = (bf16[2,4,128,256]{3,2,1,0:T(8,128)(2,1)}, f32[26,256]{1,0:T(8,128)}) custom-call(bf16[4,512,256]{2,1,0:T(8,128)(2,1)} %bitcast.12, bf16[4,2,128,256]{3,2,1,0:T(8,128)(2,1)} %bitcast.13, bf16[4,2,128,1024]{3,2,1,0:T(8,128)(2,1)} %feat_hbm.1, bf16[18,256,256]{2,1,0:T(8,128)(2,1)} %bitcast.11, bf16[9,128,512]{2,1,0:T(8,128)(2,1)} %constant.6.clone.send_hbm, ...), custom_call_target="tpu_custom_call" | custom-call | flops 3000000000 | bytes 9000000 | tf_op jit(solution)/shard_map/head_backward/pallas_call | solution.py:393
  65.9 0.0 copy-done
  65.9 1.8 %convert_bitcast_fusion = bf16[4,2,128,1024]{3,2,0,1:T(8,128)(2,1)S(1)} fusion(bf16[2,4,128,256]{3,2,1,0:T(8,128)(2,1)} %get-tuple-element.4, bf16[2,1024,256]{2,1,0:T(8,128)(2,1)S(1)} %copy-done), kind=kOutput, calls=%fused_computation | convolution fusion | flops 537919488 | bytes 3670016 | tf_op jit(solution)/shard_map/kinc,kdc->iknd/dot_general | solution.py:426
  67.7 0.0 copy-start.1
  67.7 1.5 %copy.10 = bf16[4,2,128,1024]{3,2,1,0:T(8,128)(2,1)} copy(bf16[4,2,128,1024]{3,2,0,1:T(8,128)(2,1)S(1)} %convert_bitcast_fusion) | data formatting | bytes 4194304
  69.2 0.0 copy-done.1
  69.2 0.6 copy.13
Async XLA Ops:
  0.6 65.2 %copy-start = (bf16[2,1024,256]{2,1,0:T(8,128)(2,1)S(1)}, bf16[2,1024,256]{2,1,0:T(8,128)(2,1)}, u32[]{:S(2)}) copy-start(bf16[2,1024,256]{2,1,0:T(8,128)(2,1)} %param.9) | copy-start | bytes 3145732
  67.7 1.5 %copy-start.1 = (f32[26,256]{1,0:T(8,128)S(1)}, f32[26,256]{1,0:T(8,128)}, u32[]{:S(2)}) copy-start(f32[26,256]{1,0:T(8,128)} %get-tuple-element.11) | copy-start | bytes 79876

commit v2 on v1

--- a/solution.py
+++ b/solution.py
@@ -101,11 +101,11 @@
 
 
 def kernel(
-    cot_hbm, saved_hbm, feat_hbm, w_hbm, send_hbm, take_hbm, order_hbm,
-    tok_out, head_out,
-    cot, saved, feat, wconv, send_m, take_m, order_m,
-    saved_t, feat_t, halo_out, halo_in, corner, acc, pooled, grad_acc, grad, tok,
-    head, send_c, recv_c, part, send_1, recv_1, send_2, recv_2, last, send_3, recv_3,
+    cot_hbm, saved_hbm, feat_hbm, w_hbm, proj_hbm, send_hbm, take_hbm, order_hbm,
+    fg_out, head_out,
+    cot, saved, feat, wconv, proj, send_m, take_m, order_m,
+    saved_t, feat_t, halo_out, halo_in, corner, acc, pooled, grad_acc, grad, tok, fg,
+    head, send_c, recv_c, part, split_1, send_1, recv_1, kept_1, split_2, send_2, recv_2, last, send_3, recv_3,
     load_sem, halo_ss, halo_rs, tok_ss, tok_rs, c_ss, c_rs, ss_1, rs_1, ss_2, rs_2, ss_3, rs_3, out_sem,
 ):
     dp = lax.axis_index("dp")
@@ -142,10 +142,43 @@
         for n, (src, dst) in enumerate([
             (cot_hbm, cot), (send_hbm.at[place], send_m), (order_hbm, order_m),
             (take_hbm.at[place], take_m), (saved_hbm, saved), (w_hbm, wconv), (feat_hbm, feat),
+            (proj_hbm, proj),
         ])
     ]
     for load in loads:
         load.start()
+
+    barrier = pltpu.get_barrier_semaphore()
+
+    def greet(device):
+        pl.semaphore_signal(barrier, inc=1, device_id=device, device_id_type=MESH)
+
+    def has(dr, dc):
+        to_row, to_col = row + dr, col + dc
+        ok = jnp.logical_and(to_row >= 0, to_row < 16)
+        return jnp.logical_and(ok, jnp.logical_and(to_col >= 0, to_col < 8))
+
+    def beside(dr, dc):
+        return jnp.clip(row + dr, 0, 15) * 8 + gray(jnp.clip(col + dc, 0, 7))
+
+    greeted = jnp.int32(0)
+    for dr, dc in DIRS:
+        if dr:
+
+            @pl.when(has(dr, dc))
+            def _():
+                greet({"tile": beside(dr, dc)})
+
+            greeted = greeted + has(dr, dc).astype(jnp.int32)
+    for n in range(1, 8):
+        greet({"tile": row * 8 + (g + n) % 8})
+    for n in range(2):
+        greet({"dp": 1 - dp, "tile": z * 16 + y * 4 + n * 2 + core})
+        greet({"tile": z * 16 + (y // 2 * 2 + 2 + n) % 4 * 4 + xh * 2 + core})
+    for n in range(1, 8):
+        for c in range(2):
+            greet({"tile": (z + n) % 8 * 16 + y * 4 + xh * 2 + c})
+    greeted = greeted + 25
 
     for n in range(3):
         loads[n].wait()
@@ -160,18 +193,12 @@
         halo_out[START[d] + 4 * MAIN[d] : START[d] + SIZE[d], :] = corners[d * 16 : d * 16 + 16]
 
     def halo(d):
-        dr, dc = DIRS[d]
-        there = jnp.clip(row + dr, 0, 15) * 8 + gray(jnp.clip(col + dc, 0, 7))
         return remote(
             halo_out.at[START[d] : START[d] + SIZE[d]], halo_in.at[START[d] : START[d] + SIZE[d]],
-            halo_ss.at[d], halo_rs.at[d], {"tile": there},
+            halo_ss.at[d], halo_rs.at[d], {"tile": beside(*DIRS[d])},
         )
 
-    def has(dr, dc):
-        to_row, to_col = row + dr, col + dc
-        ok = jnp.logical_and(to_row >= 0, to_row < 16)
-        return jnp.logical_and(ok, jnp.logical_and(to_col >= 0, to_col < 8))
-
+    pl.semaphore_wait(barrier, greeted)
     for d in range(8):
         dr, dc = DIRS[d]
 
@@ -238,97 +265,137 @@
 
     mine = pl.ds(pl.multiple_of(core * 128, 128), 128)
     theirs = pl.ds(pl.multiple_of((1 - core) * 128, 128), 128)
-    pair = {"tile": tile + 1 - 2 * core}
+    pair_device = {"tile": tile + 1 - 2 * core}
 
     def swap(q):
-        return remote(send_c.at[q], recv_c.at[q], c_ss.at[q], c_rs.at[q], pair)
-
-    def first(q, to_a):
-        slot = (to_a - a + 4) % 4
+        return remote(send_c.at[q], recv_c.at[q], c_ss.at[q], c_rs.at[q], pair_device)
+
+    def to_first(pair, n):
+        return jnp.where(core == 0, pair // 4 + n % 2 * 2, n)
+
+    def first(pair, n):
+        to_a = to_first(pair, n)
+        slot = jnp.where(core == 0, pair % 4 * 2 + n // 2, pair)
+        step = (to_a - a + 3) % 4
         return remote(
-            send_1.at[q], recv_1.at[q // 4, slot - 1], ss_1.at[q], rs_1.at[q // 4, slot - 1], in_plane(to_a, b)
+            send_1.at[pair, n], recv_1.at[slot, step], ss_1.at[pair, n], rs_1.at[slot, step], in_plane(to_a, b)
         )
 
     def ready(q):
         send_c[q] = head[q * CHUNK : (q + 1) * CHUNK, theirs].astype(BF)
         swap(q).start()
 
-    def reduced(q):
-        swap(q).wait_recv()
-        total = head[q * CHUNK : (q + 1) * CHUNK, mine] + recv_c[q].astype(F32)
-        part[q] = total
-        send_1[q] = total.astype(BF)
-
-        @pl.when(a != q % 4)
-        def _():
-            first(q, q % 4).start()
-
-    for k in range(2):
+    def reduced(pair):
+        for q in (2 * pair, 2 * pair + 1):
+            swap(q).wait_recv()
+            part[q] = head[q * CHUNK : (q + 1) * CHUNK, mine] + recv_c[q].astype(F32)
+
+        @pl.when(core == 0)
+        def _():
+            for n in range(4):
+                for p in range(4):
+                    at = p * 104 + n % 2 * 52
+                    split_1[pair, n, p * 52 : p * 52 + 52, :] = part[2 * pair + n // 2, at : at + 52, :]
+
+        @pl.when(core == 1)
+        def _():
+            for n in range(4):
+                for h in range(2):
+                    split_1[pair, n, h * 104 : h * 104 + 104, :] = part[2 * pair + h, n * 104 : n * 104 + 104, :]
+
+        for n in range(4):
+            send_1[pair, n] = split_1[pair, n].astype(BF)
+
+            @pl.when(a != to_first(pair, n))
+            def _():
+                first(pair, n).start()
+
+    for k in (1, 0):
         for t in range(9):
             at = 2048 + (k * 9 + t) * 256
             head[at : at + 256, :] = mm(saved_t[k * 256 : (k + 1) * 256, :], tap(t))
-        for q in (range(5, 10), range(10, 16))[k]:
+        for q in (range(5, 11), range(11, 16))[k]:
             ready(q)
     loads[6].wait()
     for k in range(2):
         for i in range(4):
             feat_t[k * 1024 : (k + 1) * 1024, i * 128 : (i + 1) * 128] = feat[i, k].T
-    for q in range(5, 16):
-        reduced(q)
+    for pair in (6, 7, 5, 4, 3):
+        reduced(pair)
 
     for n in range(1, 8):
         regroup(n).wait_recv()
-    out_copy = pltpu.make_async_copy(tok, tok_out, out_sem)
-    out_copy.start()
     for k in range(2):
         for h in range(4):
             at = k * 1024 + h * 256
             head[at : at + 256, :] = mm(feat_t[at : at + 256, :], tok[k].reshape(512, 256))
         for q in (range(0, 2), range(2, 5))[k]:
             ready(q)
-    for q in range(0, 5):
-        reduced(q)
+    for pair in (0, 1, 2):
+        reduced(pair)
+
+    loads[7].wait()
+    for i in range(4):
+        for k in range(2):
+            fg[i, k] = mm_t(tok[k, i], proj[k]).astype(BF)
+    out_copy = pltpu.make_async_copy(fg, fg_out, out_sem)
+    out_copy.start()
 
     def second(to_b):
-        slot = (to_b - b + 4) % 4
+        step = (to_b - b + 3) % 4
         return remote(
-            send_2.at[to_b], recv_2.at[slot - 1], ss_2.at[slot - 1], rs_2.at[slot - 1], in_plane(a, to_b)
+            send_2.at[to_b], recv_2.at[step], ss_2.at[step], rs_2.at[step], in_plane(a, to_b)
         )
 
-    for j in (3, 2, 1, 0):
-        total = part[j * 4 + a]
+    for e in (7, 6, 5, 4, 3, 2, 1, 0):
+        pair = jnp.where(core == 0, a % 2 * 4 + e // 2, e)
+        n = jnp.where(core == 0, e % 2 * 2 + a // 2, a)
+        total = split_1[pair, n]
         for s in range(3):
-            first(j * 4 + 0, (a + s + 1) % 4).wait_recv()
-            total = total + recv_1[j, s].astype(F32)
-        part[j * 4 + a] = total
-        send_2[j] = total.astype(BF)
+            remote(
+                send_1.at[0, 0], recv_1.at[e, s], ss_1.at[0, 0], rs_1.at[e, s], pair_device
+            ).wait_recv()
+            total = total + recv_1[e, s].astype(F32)
+        kept_1[e] = total
+
+    @pl.when(core == 0)
+    def _():
+        for j in range(4):
+            for e in range(8):
+                split_2[j, e * 52 : e * 52 + 52, :] = kept_1[e, j * 52 : j * 52 + 52, :]
+
+    @pl.when(core == 1)
+    def _():
+        for j in range(4):
+            for p in range(8):
+                at = p % 2 * 104 + j // 2 * 52
+                split_2[j, p * 52 : p * 52 + 52, :] = kept_1[j % 2 * 4 + p // 2, at : at + 52, :]
+
+    for j in range(4):
+        send_2[j] = split_2[j].astype(BF)
 
         @pl.when(b != j)
         def _():
             second(j).start()
 
-    total = part[b * 4 + a]
+    total = split_2[b]
     for s in range(3):
         second((b + s + 1) % 4).wait_recv()
         total = total + recv_2[s].astype(F32)
     last[0:CHUNK, :] = total
     last[CHUNK:432, :] = jnp.zeros((16, 128), F32)
-    for p in range(16):
-        send_3[p] = last[p * HEAD_ROWS : p * HEAD_ROWS + 32, :].astype(BF)
-
-    held = b * 4 + a
-    own = dp * 8 + z
 
     def third(p):
         return remote(
             send_3.at[p], recv_3.at[z, core], ss_3.at[p], rs_3.at[z, core],
-            {"dp": held // 8, "tile": held % 8 * 16 + p},
+            {"tile": p // 2 * 16 + y * 4 + xh * 2 + p % 2},
         )
 
     def to_self(p):
-        return jnp.logical_and(held == own, tile % 16 == p)
+        return jnp.logical_and(z == p // 2, core == p % 2)
 
     for p in range(16):
+        send_3[p] = last[p * HEAD_ROWS : p * HEAD_ROWS + 32, :].astype(BF)
 
         @pl.when(jnp.logical_not(to_self(p)))
         def _():
@@ -338,26 +405,19 @@
         def _():
             recv_3[z, core] = send_3[p]
 
-    total = [None, None]
-    for cc in range(2):
-        from_x = own % 4 if cc == 0 else own // 4
-        from_y = own // 4 if cc == 0 else own % 4
+    scale = 1.0 / math.sqrt(8 * 16384)
+    for c in range(2):
+        total = jnp.zeros((32, 128), F32)
         for zz in range(8):
-            source = zz * 16 + from_y * 4 + from_x // 2 * 2 + cc
-            itself = jnp.logical_and(from_x % 2 == dp, source == tile)
-
-            @pl.when(jnp.logical_not(itself))
+
+            @pl.when(jnp.logical_not(to_self(zz * 2 + c)))
             def _():
                 remote(
-                    send_3.at[0], recv_3.at[zz, cc], ss_3.at[0], rs_3.at[zz, cc],
-                    {"dp": from_x % 2, "tile": source},
+                    send_3.at[0], recv_3.at[zz, c], ss_3.at[0], rs_3.at[zz, c], pair_device
                 ).wait_recv()
 
-            piece = recv_3[zz, cc].astype(F32)
-            total[cc] = piece if zz == 0 else total[cc] + piece
-    scale = 1.0 / math.sqrt(8 * 16384)
-    for cc in range(2):
-        head_out[:, cc * 128 : (cc + 1) * 128] = total[cc][:HEAD_ROWS] * scale
+            total = total + recv_3[zz, c].astype(F32)
+        head_out[:, c * 128 : (c + 1) * 128] = total[:HEAD_ROWS] * scale
 
     for d in range(8):
 
@@ -369,10 +429,12 @@
         regroup(n).wait_send()
     for q in range(16):
         swap(q).wait_send()
-
-        @pl.when(a != q % 4)
-        def _():
-            first(q, q % 4).wait_send()
+    for pair in range(8):
+        for n in range(4):
+
+            @pl.when(a != to_first(pair, n))
+            def _():
+                first(pair, n).wait_send()
 
     for s in range(3):
         second((b + s + 1) % 4).wait_send()
@@ -390,41 +452,45 @@
     hbm = pl.BlockSpec(memory_space=pl.ANY)
     dma = pltpu.SemaphoreType.DMA
     vmem = pltpu.VMEM
-    tok, head = pl.pallas_call(
+    return pl.pallas_call(
         kernel,
         out_shape=(
-            jax.ShapeDtypeStruct((2, 4, 128, 256), BF),
+            jax.ShapeDtypeStruct((4, 2, 128, 1024), BF),
             jax.ShapeDtypeStruct((HEAD_ROWS, 256), F32),
         ),
-        in_specs=[hbm] * 7,
+        in_specs=[hbm] * 8,
         out_specs=(hbm, pl.BlockSpec(memory_space=pltpu.VMEM)),
         scratch_shapes=[
             vmem((4, 512, 256), BF), vmem((4, 2, 128, 256), BF), vmem((4, 2, 128, 1024), BF),
-            vmem((18, 256, 256), BF), vmem((128, 512), BF), vmem((480, 640), BF), vmem((2, 128, 128), BF),
+            vmem((18, 256, 256), BF), vmem((2, 1024, 256), BF),
+            vmem((128, 512), BF), vmem((480, 640), BF), vmem((2, 128, 128), BF),
             vmem((512, 512), BF), vmem((2048, 512), BF), vmem((512, 256), BF), vmem((512, 256), BF),
             vmem((128, 256), BF), vmem((4, 480, 256), F32), vmem((3, 4, 160, 256), BF),
             vmem((512, 256), F32), vmem((2, 4, 128, 256), BF), vmem((2, 4, 128, 256), BF),
+            vmem((4, 2, 128, 1024), BF),
             vmem((6656, 256), F32), vmem((16, CHUNK, 128), BF), vmem((16, CHUNK, 128), BF),
-            vmem((16, CHUNK, 128), F32), vmem((16, CHUNK, 128), BF), vmem((4, 3, CHUNK, 128), BF),
+            vmem((16, CHUNK, 128), F32), vmem((8, 4, 208, 128), F32), vmem((8, 4, 208, 128), BF),
+            vmem((8, 3, 208, 128), BF), vmem((8, 208, 128), F32), vmem((4, CHUNK, 128), F32),
             vmem((4, CHUNK, 128), BF), vmem((3, CHUNK, 128), BF), vmem((432, 128), F32),
             vmem((16, 32, 128), BF), vmem((8, 2, 32, 128), BF),
-            dma((7,)), dma((8,)), dma((8,)), dma((8,)), dma((8,)), dma((16,)), dma((16,)),
-            dma((16,)), dma((4, 3)), dma((3,)), dma((3,)), dma((16,)), dma((8, 2)), dma,
+            dma((8,)), dma((8,)), dma((8,)), dma((8,)), dma((8,)), dma((16,)), dma((16,)),
+            dma((8, 4)), dma((8, 3)), dma((3,)), dma((3,)), dma((16,)), dma((8, 2)), dma,
         ],
-        compiler_params=pltpu.CompilerParams(has_side_effects=True, vmem_limit_bytes=56 * 2**20),
-        cost_estimate=pl.CostEstimate(flops=3_000_000_000, bytes_accessed=9_000_000, transcendentals=0),
+        compiler_params=pltpu.CompilerParams(
+            collective_id=0, has_side_effects=True, vmem_limit_bytes=56 * 2**20
+        ),
+        cost_estimate=pl.CostEstimate(flops=3_500_000_000, bytes_accessed=11_000_000, transcendentals=0),
         name="head_backward",
     )(
         cotangent.reshape(4, 512, 256),
         saved.reshape(4, 2, 128, 256),
         features,
         conv_weight.reshape(18, 256, 256),
+        proj_weight,
         send,
         take,
         order,
     )
-    feature_grad = jnp.einsum("kinc,kdc->iknd", tok, proj_weight, preferred_element_type=F32)
-    return feature_grad.astype(BF), head
 
 
 def solution(mesh):

time: 70.5 us -> 58.4 us (0.83)
  Pallas kernels: 65.2 us -> 53.9 us
  matrix products: 1.78 us -> 0 us
  local copies, waits for them, and re-layouts: 2.12 us -> 3.7 us
    pallas_call x1, Pallas kernels: 65.2 us -> 53.9 us  [per_device(): pl.pallas_call(kernel, out_shape=(jax.ShapeDtypeStruct((4, 2, 128, 1024),...]
    dot_general x1 -> x0, matrix products: 1.78 us -> none  [per_device(): jnp.einsum('kinc,kdc->iknd', tok, proj_weight, preferred_element_type=F32)]
    unnamed x6 -> x4, local copies, waits for them, and re-layouts: 2.12 us -> 3.7 us
where the time goes in v2:
time: 58.4 us; the launch traced here: 58.3 us
  Pallas kernels  53.9 us (92%)
  local copies, waits for them, and re-layouts  3.7 us (6%)
  between operations  0.65 us (1%)
    pallas_call x1, Pallas kernels, per_device(): pl.pallas_call(kernel, out_shape=(jax.ShapeDtypeStruct((4, 2, 128, 1024),...  53.9 us
    unnamed x4, local copies, waits for them, and re-layouts  3.7 us

profile of v2, /device:TPU:1, one launch (start us, length us, event | category | flops | bytes accessed | tf_op | source)
XLA Modules:
  0.0 58.3 jit_solution(16140075203413939992)
XLA Ops:
  0.6 53.9 %head_backward.1 = (bf16[4,2,128,1024]{3,2,1,0:T(8,128)(2,1)}, f32[26,256]{1,0:T(8,128)}) custom-call(bf16[4,512,256]{2,1,0:T(8,128)(2,1)} %bitcast.4, bf16[4,2,128,256]{3,2,1,0:T(8,128)(2,1)} %bitcast.5, bf16[4,2,128,1024]{3,2,1,0:T(8,128)(2,1)} %feat_hbm.1, bf16[18,256,256]{2,1,0:T(8,128)(2,1)} %bitcast.3, bf16[2,1024,256]{2,1,0:T(8,128)(2,1)} %proj_hbm.1, ...), custom_call_target="tpu_custom_call" | custom-call | flops 3500000000 | bytes 11000000 | tf_op jit(solution)/shard_map/head_backward/pallas_call | solution.py:455
  54.6 0.0 copy-start
  54.6 3.1 %copy.12 = bf16[4,2,128,1024]{3,2,1,0:T(8,128)(2,1)} copy(bf16[4,2,128,1024]{3,2,1,0:T(8,128)(2,1)} %get-tuple-element.4) | data formatting | bytes 4194304
  57.7 0.0 copy-done
  57.7 0.6 %copy.13 = f32[26,256]{1,0:T(8,128)} copy(f32[26,256]{1,0:T(8,128)S(1)} %copy-done) | data formatting | bytes 53248
Async XLA Ops:
  54.6 3.1 %copy-start = (f32[26,256]{1,0:T(8,128)S(1)}, f32[26,256]{1,0:T(8,128)}, u32[]{:S(2)}) copy-start(f32[26,256]{1,0:T(8,128)} %get-tuple-element.5) | copy-start | bytes 79876

commit v3 on v2

--- a/solution.py
+++ b/solution.py
@@ -101,11 +101,11 @@
 
 
 def kernel(
-    cot_hbm, saved_hbm, feat_hbm, w_hbm, proj_hbm, send_hbm, take_hbm, order_hbm,
-    fg_out, head_out,
-    cot, saved, feat, wconv, proj, send_m, take_m, order_m,
-    saved_t, feat_t, halo_out, halo_in, corner, acc, pooled, grad_acc, grad, tok, fg,
-    head, send_c, recv_c, part, split_1, send_1, recv_1, kept_1, split_2, send_2, recv_2, last, send_3, recv_3,
+    cot_hbm, saved_hbm, feat_hbm, w_hbm, send_hbm, take_hbm, order_hbm,
+    tok_out, head_out,
+    cot, saved, feat, wconv, send_m, take_m, order_m,
+    saved_t, feat_t, halo_out, halo_in, corner, acc, pooled, grad_acc, grad, tok,
+    head, send_c, recv_c, part, split_1, send_1, recv_1, split_2, send_2, recv_2, kept, last, send_3, recv_3,
     load_sem, halo_ss, halo_rs, tok_ss, tok_rs, c_ss, c_rs, ss_1, rs_1, ss_2, rs_2, ss_3, rs_3, out_sem,
 ):
     dp = lax.axis_index("dp")
@@ -142,7 +142,6 @@
         for n, (src, dst) in enumerate([
             (cot_hbm, cot), (send_hbm.at[place], send_m), (order_hbm, order_m),
             (take_hbm.at[place], take_m), (saved_hbm, saved), (w_hbm, wconv), (feat_hbm, feat),
-            (proj_hbm, proj),
         ])
     ]
     for load in loads:
@@ -240,8 +239,16 @@
         u, v = t // 3, t % 3
         return pooled[2 - v, :, (2 - u) * 16 : (2 - u) * 16 + 128, :].reshape(512, 256)
 
+    def regroup(k, n):
+        there = (g + n) % 8
+        return remote(
+            grad.at[k, :, pl.ds(pl.multiple_of(there * 16, 16), 16)],
+            tok.at[k, :, pl.ds(pl.multiple_of(col * 16, 16), 16)],
+            tok_ss.at[k, n], tok_rs.at[k, n], {"tile": row * 8 + there},
+        )
+
     loads[5].wait()
-    for k in range(2):
+    for k in (1, 0):
         for t in range(9):
             term = mm_t(tap(t), wconv[k * 9 + t])
             if t == 0:
@@ -250,18 +257,9 @@
                 grad_acc[...] += term
             else:
                 grad[k] = (grad_acc[...] + term).astype(BF).reshape(4, 128, 256)
-
-    def regroup(n):
-        there = (g + n) % 8
-        return remote(
-            grad.at[:, :, pl.ds(pl.multiple_of(there * 16, 16), 16)],
-            tok.at[:, :, pl.ds(pl.multiple_of(col * 16, 16), 16)],
-            tok_ss.at[n], tok_rs.at[n], {"tile": row * 8 + there},
-        )
-
-    for n in range(1, 8):
-        regroup(n).start()
-    tok[:, :, pl.ds(pl.multiple_of(col * 16, 16), 16)] = grad[:, :, pl.ds(pl.multiple_of(g * 16, 16), 16)]
+        for n in range(1, 8):
+            regroup(k, n).start()
+        tok[k, :, pl.ds(pl.multiple_of(col * 16, 16), 16)] = grad[k, :, pl.ds(pl.multiple_of(g * 16, 16), 16)]
 
     mine = pl.ds(pl.multiple_of(core * 128, 128), 128)
     theirs = pl.ds(pl.multiple_of((1 - core) * 128, 128), 128)
@@ -309,6 +307,73 @@
             @pl.when(a != to_first(pair, n))
             def _():
                 first(pair, n).start()
+
+    def second(j, to_b):
+        step = (to_b - b + 3) % 4
+        return remote(
+            send_2.at[j, to_b], recv_2.at[j, step], ss_2.at[j, to_b], rs_2.at[j, step], in_plane(a, to_b)
+        )
+
+    def to_second(j):
+        for h in range(2):
+            e = jnp.where(core == 0, 2 * j + h, j + 4 * h)
+            pair = jnp.where(core == 0, a % 2 * 4 + j, e)
+            n = jnp.where(core == 0, h * 2 + a // 2, a)
+            total = split_1[pair, n]
+            for s in range(3):
+                remote(
+                    send_1.at[0, 0], recv_1.at[e, s], ss_1.at[0, 0], rs_1.at[e, s], pair_device
+                ).wait_recv()
+                total = total + recv_1[e, s].astype(F32)
+            kept[j, h] = total
+
+        @pl.when(core == 0)
+        def _():
+            for to_b in range(4):
+                for h in range(2):
+                    split_2[j, to_b, h * 52 : h * 52 + 52, :] = kept[j, h, to_b * 52 : to_b * 52 + 52, :]
+
+        @pl.when(core == 1)
+        def _():
+            for to_b in range(4):
+                for h in range(2):
+                    at = h * 104 + to_b // 2 * 52
+                    split_2[j, to_b, h * 52 : h * 52 + 52, :] = kept[j, to_b % 2, at : at + 52, :]
+
+        for to_b in range(4):
+            split_2[j, to_b, 104:112, :] = jnp.zeros((8, 128), F32)
+            send_2[j, to_b] = split_2[j, to_b].astype(BF)
+
+            @pl.when(b != to_b)
+            def _():
+                second(j, to_b).start()
+
+    def third(p):
+        return remote(
+            send_3.at[p], recv_3.at[z, core], ss_3.at[p], rs_3.at[z, core],
+            {"tile": p // 2 * 16 + y * 4 + xh * 2 + p % 2},
+        )
+
+    def to_self(p):
+        return jnp.logical_and(z == p // 2, core == p % 2)
+
+    def to_third(j):
+        total = split_2[j, b]
+        for s in range(3):
+            second(j, (b + s + 1) % 4).wait_recv()
+            total = total + recv_2[j, s].astype(F32)
+        last[j] = total
+        for n in range(4):
+            p = 4 * j + n
+            send_3[p] = last[j, n * HEAD_ROWS : n * HEAD_ROWS + 32, :].astype(BF)
+
+            @pl.when(jnp.logical_not(to_self(p)))
+            def _():
+                third(p).start()
+
+            @pl.when(to_self(p))
+            def _():
+                recv_3[z, core] = send_3[p]
 
     for k in (1, 0):
         for t in range(9):
@@ -320,92 +385,31 @@
     for k in range(2):
         for i in range(4):
             feat_t[k * 1024 : (k + 1) * 1024, i * 128 : (i + 1) * 128] = feat[i, k].T
-    for pair in (6, 7, 5, 4, 3):
+    for pair in (7, 3, 6, 5, 4):
         reduced(pair)
 
-    for n in range(1, 8):
-        regroup(n).wait_recv()
-    for k in range(2):
+    for k in (1, 0):
+        for n in range(1, 8):
+            regroup(k, n).wait_recv()
         for h in range(4):
             at = k * 1024 + h * 256
             head[at : at + 256, :] = mm(feat_t[at : at + 256, :], tok[k].reshape(512, 256))
-        for q in (range(0, 2), range(2, 5))[k]:
+        for q in (range(0, 3), range(3, 5))[k]:
             ready(q)
-    for pair in (0, 1, 2):
-        reduced(pair)
-
-    loads[7].wait()
-    for i in range(4):
-        for k in range(2):
-            fg[i, k] = mm_t(tok[k, i], proj[k]).astype(BF)
-    out_copy = pltpu.make_async_copy(fg, fg_out, out_sem)
+    out_copy = pltpu.make_async_copy(tok, tok_out, out_sem)
     out_copy.start()
-
-    def second(to_b):
-        step = (to_b - b + 3) % 4
-        return remote(
-            send_2.at[to_b], recv_2.at[step], ss_2.at[step], rs_2.at[step], in_plane(a, to_b)
-        )
-
-    for e in (7, 6, 5, 4, 3, 2, 1, 0):
-        pair = jnp.where(core == 0, a % 2 * 4 + e // 2, e)
-        n = jnp.where(core == 0, e % 2 * 2 + a // 2, a)
-        total = split_1[pair, n]
-        for s in range(3):
-            remote(
-                send_1.at[0, 0], recv_1.at[e, s], ss_1.at[0, 0], rs_1.at[e, s], pair_device
-            ).wait_recv()
-            total = total + recv_1[e, s].astype(F32)
-        kept_1[e] = total
-
-    @pl.when(core == 0)
-    def _():
-        for j in range(4):
-            for e in range(8):
-                split_2[j, e * 52 : e * 52 + 52, :] = kept_1[e, j * 52 : j * 52 + 52, :]
-
-    @pl.when(core == 1)
-    def _():
-        for j in range(4):
-            for p in range(8):
-                at = p % 2 * 104 + j // 2 * 52
-                split_2[j, p * 52 : p * 52 + 52, :] = kept_1[j % 2 * 4 + p // 2, at : at + 52, :]
-
-    for j in range(4):
-        send_2[j] = split_2[j].astype(BF)
-
-        @pl.when(b != j)
-        def _():
-            second(j).start()
-
-    total = split_2[b]
-    for s in range(3):
-        second((b + s + 1) % 4).wait_recv()
-        total = total + recv_2[s].astype(F32)
-    last[0:CHUNK, :] = total
-    last[CHUNK:432, :] = jnp.zeros((16, 128), F32)
-
-    def third(p):
-        return remote(
-            send_3.at[p], recv_3.at[z, core], ss_3.at[p], rs_3.at[z, core],
-            {"tile": p // 2 * 16 + y * 4 + xh * 2 + p % 2},
-        )
-
-    def to_self(p):
-        return jnp.logical_and(z == p // 2, core == p % 2)
-
-    for p in range(16):
-        send_3[p] = last[p * HEAD_ROWS : p * HEAD_ROWS + 32, :].astype(BF)
-
-        @pl.when(jnp.logical_not(to_self(p)))
-        def _():
-            third(p).start()
-
-        @pl.when(to_self(p))
-        def _():
-            recv_3[z, core] = send_3[p]
-
-    scale = 1.0 / math.sqrt(8 * 16384)
+    reduced(2)
+    to_second(3)
+    reduced(1)
+    reduced(0)
+    to_third(3)
+    to_second(2)
+    to_second(1)
+    to_third(2)
+    to_second(0)
+    to_third(1)
+    to_third(0)
+
     for c in range(2):
         total = jnp.zeros((32, 128), F32)
         for zz in range(8):
@@ -417,7 +421,7 @@
                 ).wait_recv()
 
             total = total + recv_3[zz, c].astype(F32)
-        head_out[:, c * 128 : (c + 1) * 128] = total[:HEAD_ROWS] * scale
+        head_out[:, c * 128 : (c + 1) * 128] = total[:HEAD_ROWS]
 
     for d in range(8):
 
@@ -425,8 +429,9 @@
         def _():
             halo(d).wait_send()
 
-    for n in range(1, 8):
-        regroup(n).wait_send()
+    for k in range(2):
+        for n in range(1, 8):
+            regroup(k, n).wait_send()
     for q in range(16):
         swap(q).wait_send()
     for pair in range(8):
@@ -436,8 +441,13 @@
             def _():
                 first(pair, n).wait_send()
 
-    for s in range(3):
-        second((b + s + 1) % 4).wait_send()
+    for j in range(4):
+        for to_b in range(4):
+
+            @pl.when(b != to_b)
+            def _():
+                second(j, to_b).wait_send()
+
     for p in range(16):
 
         @pl.when(jnp.logical_not(to_self(p)))
@@ -445,52 +455,88 @@
             third(p).wait_send()
 
     out_copy.wait()
+
+
+def finish(tok_hbm, proj_hbm, head_in, fg_hbm, head_out, tok, proj, fg, load_sem, out_sem):
+    loads = [
+        pltpu.make_async_copy(src.at[k], dst.at[k], load_sem.at[2 * n + k])
+        for k in range(2)
+        for n, (src, dst) in enumerate([(tok_hbm, tok), (proj_hbm, proj)])
+    ]
+    for load in loads:
+        load.start()
+    head_out[...] = head_in[...] * (1.0 / math.sqrt(8 * 16384))
+    outs = []
+    for k in range(2):
+        loads[2 * k].wait()
+        loads[2 * k + 1].wait()
+        for i in range(4):
+            fg[i, k] = mm_t(tok[k, i], proj[k]).astype(BF)
+            outs.append(pltpu.make_async_copy(fg.at[i, k], fg_hbm.at[i, k], out_sem.at[i, k]))
+            outs[-1].start()
+    for out in outs:
+        out.wait()
 
 
 def per_device(features, proj_weight, conv_weight, saved, cotangent):
     send, take, order = (jnp.asarray(t) for t in tables())
     hbm = pl.BlockSpec(memory_space=pl.ANY)
+    whole = pl.BlockSpec(memory_space=pltpu.VMEM)
     dma = pltpu.SemaphoreType.DMA
     vmem = pltpu.VMEM
-    return pl.pallas_call(
+    tok, head = pl.pallas_call(
         kernel,
         out_shape=(
-            jax.ShapeDtypeStruct((4, 2, 128, 1024), BF),
+            jax.ShapeDtypeStruct((2, 4, 128, 256), BF),
             jax.ShapeDtypeStruct((HEAD_ROWS, 256), F32),
         ),
-        in_specs=[hbm] * 8,
-        out_specs=(hbm, pl.BlockSpec(memory_space=pltpu.VMEM)),
+        in_specs=[hbm] * 7,
+        out_specs=(hbm, whole),
         scratch_shapes=[
             vmem((4, 512, 256), BF), vmem((4, 2, 128, 256), BF), vmem((4, 2, 128, 1024), BF),
-            vmem((18, 256, 256), BF), vmem((2, 1024, 256), BF),
+            vmem((18, 256, 256), BF),
             vmem((128, 512), BF), vmem((480, 640), BF), vmem((2, 128, 128), BF),
             vmem((512, 512), BF), vmem((2048, 512), BF), vmem((512, 256), BF), vmem((512, 256), BF),
             vmem((128, 256), BF), vmem((4, 480, 256), F32), vmem((3, 4, 160, 256), BF),
             vmem((512, 256), F32), vmem((2, 4, 128, 256), BF), vmem((2, 4, 128, 256), BF),
-            vmem((4, 2, 128, 1024), BF),
             vmem((6656, 256), F32), vmem((16, CHUNK, 128), BF), vmem((16, CHUNK, 128), BF),
             vmem((16, CHUNK, 128), F32), vmem((8, 4, 208, 128), F32), vmem((8, 4, 208, 128), BF),
-            vmem((8, 3, 208, 128), BF), vmem((8, 208, 128), F32), vmem((4, CHUNK, 128), F32),
-            vmem((4, CHUNK, 128), BF), vmem((3, CHUNK, 128), BF), vmem((432, 128), F32),
+            vmem((8, 3, 208, 128), BF), vmem((4, 4, 112, 128), F32), vmem((4, 4, 112, 128), BF),
+            vmem((4, 3, 112, 128), BF), vmem((4, 2, 208, 128), F32), vmem((4, 112, 128), F32),
             vmem((16, 32, 128), BF), vmem((8, 2, 32, 128), BF),
-            dma((8,)), dma((8,)), dma((8,)), dma((8,)), dma((8,)), dma((16,)), dma((16,)),
-            dma((8, 4)), dma((8, 3)), dma((3,)), dma((3,)), dma((16,)), dma((8, 2)), dma,
+            dma((7,)), dma((8,)), dma((8,)), dma((2, 8)), dma((2, 8)), dma((16,)), dma((16,)),
+            dma((8, 4)), dma((8, 3)), dma((4, 4)), dma((4, 3)), dma((16,)), dma((8, 2)), dma,
         ],
         compiler_params=pltpu.CompilerParams(
             collective_id=0, has_side_effects=True, vmem_limit_bytes=56 * 2**20
         ),
-        cost_estimate=pl.CostEstimate(flops=3_500_000_000, bytes_accessed=11_000_000, transcendentals=0),
+        cost_estimate=pl.CostEstimate(flops=3_000_000_000, bytes_accessed=9_000_000, transcendentals=0),
         name="head_backward",
     )(
         cotangent.reshape(4, 512, 256),
         saved.reshape(4, 2, 128, 256),
         features,
         conv_weight.reshape(18, 256, 256),
-        proj_weight,
         send,
         take,
         order,
     )
+    return pl.pallas_call(
+        finish,
+        out_shape=(
+            jax.ShapeDtypeStruct((4, 2, 128, 1024), BF),
+            jax.ShapeDtypeStruct((HEAD_ROWS, 256), F32),
+        ),
+        in_specs=[hbm, hbm, whole],
+        out_specs=(hbm, whole),
+        scratch_shapes=[
+            vmem((2, 4, 128, 256), BF), vmem((2, 1024, 256), BF), vmem((4, 2, 128, 1024), BF),
+            dma((4,)), dma((4, 2)),
+        ],
+        compiler_params=pltpu.CompilerParams(vmem_limit_bytes=62 * 2**20),
+        cost_estimate=pl.CostEstimate(flops=540_000_000, bytes_accessed=3_600_000, transcendentals=0),
+        name="feature_grad",
+    )(tok, proj_weight, head)
 
 
 def solution(mesh):

time: 58.4 us -> 57 us (0.976)
  local copies, waits for them, and re-layouts: 3.7 us -> 0 us
  Pallas kernels: 53.9 us -> 56.2 us
    unnamed x4 -> x0, local copies, waits for them, and re-layouts: 3.7 us -> none
    pallas_call x1 -> x2, Pallas kernels: 53.9 us -> 56.2 us  [the longest x1 51.3 us: per_device(): pl.pallas_call(kernel, out_shape=(jax.ShapeDtypeStruct((2, 4, 128, 256),...]
where the time goes in v3:
time: 57 us; the launch traced here: 56.8 us
  Pallas kernels  56.2 us (99%)
  between operations  0.64 us (1%)
    pallas_call x1, Pallas kernels, per_device(): pl.pallas_call(kernel, out_shape=(jax.ShapeDtypeStruct((2, 4, 128, 256),...  51.3 us
    pallas_call x1, Pallas kernels, per_device(): pl.pallas_call(finish, out_shape=(jax.ShapeDtypeStruct((4, 2, 128, 1024),...  4.93 us

profile of v3, /device:TPU:1, one launch (start us, length us, event | category | flops | bytes accessed | tf_op | source)
XLA Modules:
  0.0 56.8 jit_solution(15467623140353471165)
XLA Ops:
  0.6 51.3 %head_backward.1 = (bf16[2,4,128,256]{3,2,1,0:T(8,128)(2,1)}, f32[26,256]{1,0:T(8,128)}) custom-call(bf16[4,512,256]{2,1,0:T(8,128)(2,1)} %bitcast.4, bf16[4,2,128,256]{3,2,1,0:T(8,128)(2,1)} %bitcast.5, bf16[4,2,128,1024]{3,2,1,0:T(8,128)(2,1)} %feat_hbm.1, bf16[18,256,256]{2,1,0:T(8,128)(2,1)} %bitcast.3, bf16[9,128,512]{2,1,0:T(8,128)(2,1)} %constant.6.clone.send_hbm, ...), custom_call_target="tpu_custom_call" | custom-call | flops 3000000000 | bytes 9000000 | tf_op jit(solution)/shard_map/head_backward/pallas_call | solution.py:487
  51.9 4.9 %feature_grad.1 = (bf16[4,2,128,1024]{3,2,1,0:T(8,128)(2,1)}, f32[26,256]{1,0:T(8,128)}) custom-call(bf16[2,4,128,256]{3,2,1,0:T(8,128)(2,1)} %get-tuple-element.4.tok_hbm, bf16[2,1024,256]{2,1,0:T(8,128)(2,1)} %proj_hbm.1, f32[26,256]{1,0:T(8,128)} %get-tuple-element.5.head_in), custom_call_target="tpu_custom_call" | custom-call | flops 540000000 | bytes 3600000 | tf_op jit(solution)/shard_map/feature_grad/pallas_call | solution.py:524

commit v4 on v3

--- a/solution.py
+++ b/solution.py
@@ -101,10 +101,10 @@
 
 
 def kernel(
-    cot_hbm, saved_hbm, feat_hbm, w_hbm, send_hbm, take_hbm, order_hbm,
-    tok_out, head_out,
-    cot, saved, feat, wconv, send_m, take_m, order_m,
-    saved_t, feat_t, halo_out, halo_in, corner, acc, pooled, grad_acc, grad, tok,
+    cot_hbm, saved_hbm, feat_hbm, w_hbm, proj_hbm, send_hbm, take_hbm, order_hbm,
+    fg_out, head_out,
+    cot, saved, feat, wconv, proj, send_m, take_m, order_m,
+    saved_t, feat_t, halo_out, halo_in, corner, acc, pooled, grad_acc, grad, tok, fg,
     head, send_c, recv_c, part, split_1, send_1, recv_1, split_2, send_2, recv_2, kept, last, send_3, recv_3,
     load_sem, halo_ss, halo_rs, tok_ss, tok_rs, c_ss, c_rs, ss_1, rs_1, ss_2, rs_2, ss_3, rs_3, out_sem,
 ):
@@ -142,9 +142,10 @@
         for n, (src, dst) in enumerate([
             (cot_hbm, cot), (send_hbm.at[place], send_m), (order_hbm, order_m),
             (take_hbm.at[place], take_m), (saved_hbm, saved), (w_hbm, wconv), (feat_hbm, feat),
+            (proj_hbm, proj),
         ])
     ]
-    for load in loads:
+    for load in loads[:4]:
         load.start()
 
     barrier = pltpu.get_barrier_semaphore()
@@ -181,6 +182,8 @@
 
     for n in range(3):
         loads[n].wait()
+    for load in loads[4:]:
+        load.start()
     for i in range(4):
         r = mm(send_m[...], cot[i]).astype(BF)
         for d in range(4):
@@ -248,7 +251,7 @@
         )
 
     loads[5].wait()
-    for k in (1, 0):
+    for k in range(2):
         for t in range(9):
             term = mm_t(tap(t), wconv[k * 9 + t])
             if t == 0:
@@ -385,30 +388,39 @@
     for k in range(2):
         for i in range(4):
             feat_t[k * 1024 : (k + 1) * 1024, i * 128 : (i + 1) * 128] = feat[i, k].T
-    for pair in (7, 3, 6, 5, 4):
+    for pair in (7, 3, 4, 5, 6):
         reduced(pair)
 
-    for k in (1, 0):
+    for k in range(2):
         for n in range(1, 8):
             regroup(k, n).wait_recv()
         for h in range(4):
             at = k * 1024 + h * 256
             head[at : at + 256, :] = mm(feat_t[at : at + 256, :], tok[k].reshape(512, 256))
-        for q in (range(0, 3), range(3, 5))[k]:
+        for q in (range(0, 2), range(2, 5))[k]:
             ready(q)
-    out_copy = pltpu.make_async_copy(tok, tok_out, out_sem)
-    out_copy.start()
-    reduced(2)
+    reduced(0)
     to_second(3)
     reduced(1)
-    reduced(0)
+    reduced(2)
+
+    loads[7].wait()
+    for k in range(2):
+        tokens = tok[k].reshape(512, 256)
+        for n in range(4):
+            fg[:, k, :, n * 256 : n * 256 + 256] = (
+                mm_t(tokens, proj[k, n * 256 : n * 256 + 256]).astype(BF).reshape(4, 128, 256)
+            )
+    out_copy = pltpu.make_async_copy(fg, fg_out, out_sem)
+    out_copy.start()
+
+    to_second(0)
     to_third(3)
+    to_second(1)
+    to_third(0)
     to_second(2)
-    to_second(1)
+    to_third(1)
     to_third(2)
-    to_second(0)
-    to_third(1)
-    to_third(0)
 
     for c in range(2):
         total = jnp.zeros((32, 128), F32)
@@ -421,7 +433,7 @@
                 ).wait_recv()
 
             total = total + recv_3[zz, c].astype(F32)
-        head_out[:, c * 128 : (c + 1) * 128] = total[:HEAD_ROWS]
+        head_out[:, c * 128 : (c + 1) * 128] = total[:HEAD_ROWS] * (1.0 / math.sqrt(8 * 16384))
 
     for d in range(8):
 
@@ -457,54 +469,34 @@
     out_copy.wait()
 
 
-def finish(tok_hbm, proj_hbm, head_in, fg_hbm, head_out, tok, proj, fg, load_sem, out_sem):
-    loads = [
-        pltpu.make_async_copy(src.at[k], dst.at[k], load_sem.at[2 * n + k])
-        for k in range(2)
-        for n, (src, dst) in enumerate([(tok_hbm, tok), (proj_hbm, proj)])
-    ]
-    for load in loads:
-        load.start()
-    head_out[...] = head_in[...] * (1.0 / math.sqrt(8 * 16384))
-    outs = []
-    for k in range(2):
-        loads[2 * k].wait()
-        loads[2 * k + 1].wait()
-        for i in range(4):
-            fg[i, k] = mm_t(tok[k, i], proj[k]).astype(BF)
-            outs.append(pltpu.make_async_copy(fg.at[i, k], fg_hbm.at[i, k], out_sem.at[i, k]))
-            outs[-1].start()
-    for out in outs:
-        out.wait()
-
-
 def per_device(features, proj_weight, conv_weight, saved, cotangent):
     send, take, order = (jnp.asarray(t) for t in tables())
-    hbm = pl.BlockSpec(memory_space=pl.ANY)
+    hbm = pl.BlockSpec(memory_space=pltpu.HBM)
     whole = pl.BlockSpec(memory_space=pltpu.VMEM)
     dma = pltpu.SemaphoreType.DMA
     vmem = pltpu.VMEM
-    tok, head = pl.pallas_call(
+    return pl.pallas_call(
         kernel,
         out_shape=(
-            jax.ShapeDtypeStruct((2, 4, 128, 256), BF),
+            jax.ShapeDtypeStruct((4, 2, 128, 1024), BF),
             jax.ShapeDtypeStruct((HEAD_ROWS, 256), F32),
         ),
-        in_specs=[hbm] * 7,
-        out_specs=(hbm, whole),
+        in_specs=[hbm] * 8,
+        out_specs=(pl.BlockSpec(memory_space=pl.ANY), whole),
         scratch_shapes=[
             vmem((4, 512, 256), BF), vmem((4, 2, 128, 256), BF), vmem((4, 2, 128, 1024), BF),
-            vmem((18, 256, 256), BF),
+            vmem((18, 256, 256), BF), vmem((2, 1024, 256), BF),
             vmem((128, 512), BF), vmem((480, 640), BF), vmem((2, 128, 128), BF),
             vmem((512, 512), BF), vmem((2048, 512), BF), vmem((512, 256), BF), vmem((512, 256), BF),
             vmem((128, 256), BF), vmem((4, 480, 256), F32), vmem((3, 4, 160, 256), BF),
             vmem((512, 256), F32), vmem((2, 4, 128, 256), BF), vmem((2, 4, 128, 256), BF),
+            vmem((4, 2, 128, 1024), BF),
             vmem((6656, 256), F32), vmem((16, CHUNK, 128), BF), vmem((16, CHUNK, 128), BF),
             vmem((16, CHUNK, 128), F32), vmem((8, 4, 208, 128), F32), vmem((8, 4, 208, 128), BF),
             vmem((8, 3, 208, 128), BF), vmem((4, 4, 112, 128), F32), vmem((4, 4, 112, 128), BF),
             vmem((4, 3, 112, 128), BF), vmem((4, 2, 208, 128), F32), vmem((4, 112, 128), F32),
             vmem((16, 32, 128), BF), vmem((8, 2, 32, 128), BF),
-            dma((7,)), dma((8,)), dma((8,)), dma((2, 8)), dma((2, 8)), dma((16,)), dma((16,)),
+            dma((8,)), dma((8,)), dma((8,)), dma((2, 8)), dma((2, 8)), dma((16,)), dma((16,)),
             dma((8, 4)), dma((8, 3)), dma((4, 4)), dma((4, 3)), dma((16,)), dma((8, 2)), dma,
         ],
         compiler_params=pltpu.CompilerParams(
@@ -517,26 +509,11 @@
         saved.reshape(4, 2, 128, 256),
         features,
         conv_weight.reshape(18, 256, 256),
+        proj_weight,
         send,
         take,
         order,
     )
-    return pl.pallas_call(
-        finish,
-        out_shape=(
-            jax.ShapeDtypeStruct((4, 2, 128, 1024), BF),
-            jax.ShapeDtypeStruct((HEAD_ROWS, 256), F32),
-        ),
-        in_specs=[hbm, hbm, whole],
-        out_specs=(hbm, whole),
-        scratch_shapes=[
-            vmem((2, 4, 128, 256), BF), vmem((2, 1024, 256), BF), vmem((4, 2, 128, 1024), BF),
-            dma((4,)), dma((4, 2)),
-        ],
-        compiler_params=pltpu.CompilerParams(vmem_limit_bytes=62 * 2**20),
-        cost_estimate=pl.CostEstimate(flops=540_000_000, bytes_accessed=3_600_000, transcendentals=0),
-        name="feature_grad",
-    )(tok, proj_weight, head)
 
 
 def solution(mesh):

time: 57 us -> 50.9 us (0.89)
  Pallas kernels: 56.2 us -> 46.4 us
  local copies, waits for them, and re-layouts: 0 us -> 3.7 us
    pallas_call x2 -> x1, Pallas kernels: 56.2 us -> 46.4 us  [per_device(): pl.pallas_call(kernel, out_shape=(jax.ShapeDtypeStruct((4, 2, 128, 1024),...]
    unnamed x0 -> x4, local copies, waits for them, and re-layouts: none -> 3.7 us
where the time goes in v4:
time: 50.9 us; the launch traced here: 50.8 us
  Pallas kernels  46.4 us (91%)
  local copies, waits for them, and re-layouts  3.7 us (7%)
  between operations  0.65 us (1%)
    pallas_call x1, Pallas kernels, per_device(): pl.pallas_call(kernel, out_shape=(jax.ShapeDtypeStruct((4, 2, 128, 1024),...  46.4 us
    unnamed x4, local copies, waits for them, and re-layouts  3.7 us

profile of v4, /device:TPU:1, one launch (start us, length us, event | category | flops | bytes accessed | tf_op | source)
XLA Modules:
  0.0 50.8 jit_solution(13727330564318138262)
XLA Ops:
  0.6 46.4 %head_backward.1 = (bf16[4,2,128,1024]{3,2,1,0:T(8,128)(2,1)}, f32[26,256]{1,0:T(8,128)}) custom-call(bf16[4,512,256]{2,1,0:T(8,128)(2,1)} %bitcast.4, bf16[4,2,128,256]{3,2,1,0:T(8,128)(2,1)} %bitcast.5, bf16[4,2,128,1024]{3,2,1,0:T(8,128)(2,1)} %feat_hbm.1, bf16[18,256,256]{2,1,0:T(8,128)(2,1)} %bitcast.3, bf16[2,1024,256]{2,1,0:T(8,128)(2,1)} %proj_hbm.1, ...), custom_call_target="tpu_custom_call" | custom-call | flops 3000000000 | bytes 9000000 | tf_op jit(solution)/shard_map/head_backward/pallas_call | solution.py:478
  47.0 0.0 copy-start
  47.0 3.1 %copy.12 = bf16[4,2,128,1024]{3,2,1,0:T(8,128)(2,1)} copy(bf16[4,2,128,1024]{3,2,1,0:T(8,128)(2,1)} %get-tuple-element.4) | data formatting | bytes 4194304
  50.1 0.0 copy-done
  50.1 0.6 %copy.13 = f32[26,256]{1,0:T(8,128)} copy(f32[26,256]{1,0:T(8,128)S(1)} %copy-done) | data formatting | bytes 53248
Async XLA Ops:
  47.0 3.1 %copy-start = (f32[26,256]{1,0:T(8,128)S(1)}, f32[26,256]{1,0:T(8,128)}, u32[]{:S(2)}) copy-start(f32[26,256]{1,0:T(8,128)} %get-tuple-element.5) | copy-start | bytes 79876

commit v5 on v4

--- a/solution.py
+++ b/solution.py
@@ -122,10 +122,13 @@
         c0, c1, c2 = c % 2, (c // 2) % 2, c // 4
         return c2 * 4 + (c2 + c1) % 2 * 2 + (c1 + c0) % 2
 
-    def in_plane(to_a, to_b):
-        to_x = jnp.where(core == 0, to_a, to_b)
-        to_y = jnp.where(core == 0, to_b, to_a)
-        return {"dp": to_x % 2, "tile": z * 16 + to_y * 4 + to_x // 2 * 2 + core}
+    beside_x, beside_y = z * 16 + y * 4 + core, z * 16 + xh * 2 + core
+
+    def in_plane(to_x, to_y, along_x):
+        return {
+            "dp": jnp.where(along_x, to_x % 2, dp),
+            "tile": jnp.where(along_x, beside_x + to_x // 2 * 2, beside_y + to_y * 4),
+        }
 
     def remote(src, dst, send_sem, recv_sem, device):
         return pltpu.make_async_remote_copy(
@@ -277,9 +280,10 @@
     def first(pair, n):
         to_a = to_first(pair, n)
         slot = jnp.where(core == 0, pair % 4 * 2 + n // 2, pair)
-        step = (to_a - a + 3) % 4
+        step = lax.rem(to_a - a + 3, 4)
         return remote(
-            send_1.at[pair, n], recv_1.at[slot, step], ss_1.at[pair, n], rs_1.at[slot, step], in_plane(to_a, b)
+            send_1.at[pair, n], recv_1.at[slot, step], ss_1.at[pair, n], rs_1.at[slot, step],
+            in_plane(pair // 4 + n % 2 * 2, n, core == 0),
         )
 
     def ready(q):
@@ -312,9 +316,10 @@
                 first(pair, n).start()
 
     def second(j, to_b):
-        step = (to_b - b + 3) % 4
+        step = lax.rem(to_b - b + 3, 4)
         return remote(
-            send_2.at[j, to_b], recv_2.at[j, step], ss_2.at[j, to_b], rs_2.at[j, step], in_plane(a, to_b)
+            send_2.at[j, to_b], recv_2.at[j, step], ss_2.at[j, to_b], rs_2.at[j, step],
+            in_plane(to_b, to_b, core == 1),
         )
 
     def to_second(j):
@@ -363,7 +368,9 @@
     def to_third(j):
         total = split_2[j, b]
         for s in range(3):
-            second(j, (b + s + 1) % 4).wait_recv()
+            remote(
+                send_2.at[0, 0], recv_2.at[j, s], ss_2.at[0, 0], rs_2.at[j, s], pair_device
+            ).wait_recv()
             total = total + recv_2[j, s].astype(F32)
         last[j] = total
         for n in range(4):
@@ -422,19 +429,6 @@
     to_third(1)
     to_third(2)
 
-    for c in range(2):
-        total = jnp.zeros((32, 128), F32)
-        for zz in range(8):
-
-            @pl.when(jnp.logical_not(to_self(zz * 2 + c)))
-            def _():
-                remote(
-                    send_3.at[0], recv_3.at[zz, c], ss_3.at[0], rs_3.at[zz, c], pair_device
-                ).wait_recv()
-
-            total = total + recv_3[zz, c].astype(F32)
-        head_out[:, c * 128 : (c + 1) * 128] = total[:HEAD_ROWS] * (1.0 / math.sqrt(8 * 16384))
-
     for d in range(8):
 
         @pl.when(has(*DIRS[d]))
@@ -467,6 +461,19 @@
             third(p).wait_send()
 
     out_copy.wait()
+
+    for c in range(2):
+        total = jnp.zeros((32, 128), F32)
+        for zz in range(8):
+
+            @pl.when(jnp.logical_not(to_self(zz * 2 + c)))
+            def _():
+                remote(
+                    send_3.at[0], recv_3.at[zz, c], ss_3.at[0], rs_3.at[zz, c], pair_device
+                ).wait_recv()
+
+            total = total + recv_3[zz, c].astype(F32)
+        head_out[:, c * 128 : (c + 1) * 128] = total[:HEAD_ROWS] * (1.0 / math.sqrt(8 * 16384))
 
 
 def per_device(features, proj_weight, conv_weight, saved, cotangent):

time: 50.9 us -> 50.7 us (level)
  no operation moved by 1% of the time
where the time goes in v5:
time: 50.7 us; the launch traced here: 50.5 us
  Pallas kernels  46.2 us (91%)
  local copies, waits for them, and re-layouts  3.7 us (7%)
  between operations  0.65 us (1%)
    pallas_call x1, Pallas kernels, per_device(): pl.pallas_call(kernel, out_shape=(jax.ShapeDtypeStruct((4, 2, 128, 1024),...  46.2 us
    unnamed x4, local copies, waits for them, and re-layouts  3.7 us

profile of v5, /device:TPU:1, one launch (start us, length us, event | category | flops | bytes accessed | tf_op | source)
XLA Modules:
  0.0 50.5 jit_solution(2298488691937106447)
XLA Ops:
  0.6 46.2 %head_backward.1 = (bf16[4,2,128,1024]{3,2,1,0:T(8,128)(2,1)}, f32[26,256]{1,0:T(8,128)}) custom-call(bf16[4,512,256]{2,1,0:T(8,128)(2,1)} %bitcast.4, bf16[4,2,128,256]{3,2,1,0:T(8,128)(2,1)} %bitcast.5, bf16[4,2,128,1024]{3,2,1,0:T(8,128)(2,1)} %feat_hbm.1, bf16[18,256,256]{2,1,0:T(8,128)(2,1)} %bitcast.3, bf16[2,1024,256]{2,1,0:T(8,128)(2,1)} %proj_hbm.1, ...), custom_call_target="tpu_custom_call" | custom-call | flops 3000000000 | bytes 9000000 | tf_op jit(solution)/shard_map/head_backward/pallas_call | solution.py:485
  46.8 0.0 copy-start
  46.8 3.1 %copy.12 = bf16[4,2,128,1024]{3,2,1,0:T(8,128)(2,1)} copy(bf16[4,2,128,1024]{3,2,1,0:T(8,128)(2,1)} %get-tuple-element.4) | data formatting | bytes 4194304
  49.9 0.0 copy-done
  49.9 0.6 %copy.13 = f32[26,256]{1,0:T(8,128)} copy(f32[26,256]{1,0:T(8,128)S(1)} %copy-done) | data formatting | bytes 53248
Async XLA Ops:
  46.8 3.1 %copy-start = (f32[26,256]{1,0:T(8,128)S(1)}, f32[26,256]{1,0:T(8,128)}, u32[]{:S(2)}) copy-start(f32[26,256]{1,0:T(8,128)} %get-tuple-element.5) | copy-start | bytes 79876
